TPU v7x, 128 devices: a whole 4x4x4 slice. The times are simulated.
128 devices in a mesh: dp: 16 (over x, y_hi, core), label: 8 (over z, y_lo).
Axes of the slice: x: 4, y: 4 (y_hi: 2, y_lo: 2; y = y_hi * 2 + y_lo), z: 4, core: 2. Of those that a mesh axis runs over, the one named last changes fastest.
Arguments:
- documents: bfloat16 [2048, 768], P('dp'), as said below
- labels: bfloat16 [262144, 768], P(('dp', 'label')), as said below
- target_owner: int32 [2048, 17, 1], P(('dp', 'label')), may hold values from 0 to 127; in each aligned block of 272 rows (0 to 271, 272 to 543, ..., all dimensions but the last counted through in order) at most 8 rows name the same one
- target_row: int32 [2048, 17], P(('dp', 'label')), may hold values from 0 to 2047
Outputs:
- doc_loss: float32 [2048], P(('dp', 'label'))
- doc_grad: float32 [2048, 768], P(('dp', 'label'))
- label_grad: float32 [262144, 768], P(('dp', 'label'))
Inputs may be any that keep to these rules, and one draw needn't show every extreme that they name: `target_owner`: within the rows of one device (aligned blocks of 16 documents with all their 17 columns) no owner is named more than 8 times, and in some block one owner is named exactly 8 times. The listed label is row target_owner * 2048 + target_row of the cache. `documents`: embedding rows. `labels`: embedding rows.
All inputs are finite; a program needn't handle non-finite values.
Results may differ from a plain program's by a relative error of at most 0.0029.
Values may be sent and summed in bfloat16 or wider, within the bound.
A program may use at most 128 MiB of HBM per device.

v0:
```python
import math

import jax
import jax.numpy as jnp
from jax import lax
from jax.sharding import PartitionSpec as P


def merged(part, axis, combine):
    gathered = jax.tree.map(lambda a: lax.all_gather(a, axis), part)

    def take(source):
        return jax.tree.map(lambda a: lax.dynamic_index_in_dim(a, source, 0, False), gathered)

    return lax.fori_loop(
        1, lax.axis_size(axis), lambda source, state: combine(state, take(source)), take(0)
    )


def stats_combine(first_stats, second_stats):
    merged_top = jnp.maximum(first_stats[0], second_stats[0])
    merged_total = first_stats[1] * jnp.exp(first_stats[0] - merged_top) + second_stats[
        1
    ] * jnp.exp(second_stats[0] - merged_top)
    return (merged_top, merged_total)


def shards(documents, labels, target_owner, target_row):
    feature_width = labels.shape[1]
    score_factor = 4.0 / math.sqrt(feature_width)
    lab_rows = labels.shape[0]
    dp_count = lax.axis_size("dp")
    label_count = lax.axis_size("label")
    devices = dp_count * label_count
    sub_rows = target_row.shape[0]
    columns = target_row.shape[1]
    requests = sub_rows * columns
    capacity = 2 * requests // devices + 4

    def block_scores(doc_piece):
        return score_factor * lax.dot_general(
            doc_piece, labels, (((1,), (1,)), ((), ())), preferred_element_type=jnp.float32
        )

    piece_scores = block_scores(lax.all_gather(documents, "dp", axis=0, tiled=True))
    piece_top = jnp.max(piece_scores, axis=1)
    piece_total = jnp.sum(jnp.exp(piece_scores - piece_top[:, None]), axis=1)
    row_top, row_total = merged((piece_top, piece_total), ("dp", "label"), stats_combine)
    log_total = row_top + jnp.log(row_total)
    doc_piece = lax.all_gather(documents, "dp", axis=0, tiled=True)
    piece_scores = block_scores(doc_piece)
    probabilities = jnp.exp(piece_scores - log_total[:, None]).astype(jnp.bfloat16)
    label_part = score_factor * lax.dot_general(
        probabilities, doc_piece, (((0,), (0,)), ((), ())), preferred_element_type=jnp.float32
    )
    doc_part = score_factor * jnp.dot(probabilities, labels, preferred_element_type=jnp.float32)
    label_sum = label_part
    label_index = lax.axis_index("label")
    global_start = (lax.axis_index("dp") * label_count + label_index) * sub_rows
    own_docs = lax.dynamic_slice_in_dim(documents, label_index * sub_rows, sub_rows, 0)
    owners = target_owner.reshape(requests)
    cache_rows = target_row.reshape(requests)
    owner_hits = (owners[:, None] == jnp.arange(devices, dtype=jnp.int32)[None, :]).astype(
        jnp.int32
    )
    earlier_hits = jnp.cumsum(owner_hits, axis=0) - owner_hits
    slot_rank = jnp.sum(earlier_hits * owner_hits, axis=1)
    send_slots = owners * capacity + slot_rank
    send_rows = (
        jnp.zeros((devices * capacity,), jnp.int32)
        .at[send_slots]
        .set(cache_rows)
        .reshape(devices, capacity)
    )
    negatives = columns - 1
    own_log_total = lax.dynamic_slice_in_dim(log_total, global_start, sub_rows, 0)
    asked_rows = lax.all_to_all(send_rows, ("dp", "label"), split_axis=0, concat_axis=0, tiled=True)
    found_rows = jnp.take(labels, asked_rows.reshape(-1), axis=0).reshape(
        asked_rows.shape[0], asked_rows.shape[1], feature_width
    )
    returned = lax.all_to_all(found_rows, ("dp", "label"), split_axis=0, concat_axis=0, tiled=True)
    fetched = jnp.take(
        returned.reshape(devices * capacity, feature_width), send_slots, axis=0
    ).reshape(sub_rows, columns, feature_width)
    target_scores = score_factor * jnp.einsum(
        "dkf,df->dk", fetched, own_docs, preferred_element_type=jnp.float32
    )
    positive = target_scores[:, 0]
    margin_gaps = target_scores[:, 1:] - positive[:, None] + 1.0
    loss_rows = own_log_total - positive + jnp.sum(jax.nn.softplus(margin_gaps), axis=1) / negatives
    weights = jax.nn.sigmoid(margin_gaps) / negatives
    coefficient = jnp.concatenate([-1.0 - jnp.sum(weights, axis=1, keepdims=True), weights], axis=1)
    doc_loss, coefficient = (loss_rows, coefficient)
    hard_grad = score_factor * jnp.sum(
        coefficient[:, :, None] * fetched.astype(jnp.float32), axis=1
    )
    row_grads = score_factor * coefficient[:, :, None] * own_docs.astype(jnp.float32)[:, None, :]
    send_grads = (
        jnp.zeros((devices * capacity, feature_width), jnp.float32)
        .at[send_slots]
        .set(row_grads.reshape(requests, feature_width))
    )
    send_grads = send_grads.reshape(devices, capacity, feature_width)
    got_grads = lax.all_to_all(send_grads, ("dp", "label"), split_axis=0, concat_axis=0, tiled=True)
    label_sum = label_sum + jax.ops.segment_sum(
        got_grads.reshape(devices * capacity, feature_width),
        asked_rows.reshape(-1),
        num_segments=lab_rows,
    )
    soft_grad = lax.psum_scatter(doc_part, ("dp", "label"), scatter_dimension=0, tiled=True)
    doc_grad = soft_grad + hard_grad
    return (doc_loss, doc_grad, label_sum)


def solution(mesh):
    return jax.shard_map(
        shards,
        mesh=mesh,
        in_specs=(
            P("dp", None),
            P(("dp", "label"), None),
            P(("dp", "label"), None, None),
            P(("dp", "label"), None),
        ),
        out_specs=(P(("dp", "label")), P(("dp", "label"), None), P(("dp", "label"), None)),
        check_vma=False,
    )
```

profile of v0, /device:TPU:0, one launch (start us, length us, event | category | flops | bytes accessed | tf_op | source)
XLA Modules:
  0.0 1468.2 jit_solution(743583679267409428)
XLA Ops:
  8.0 57.2 %all-gather.6.cloned.1.call-done = bf16[2048,768]{1,0:T(8,128)(2,1)} async-done(((bf16[128,768]{1,0:T(8,128)(2,1)}), bf16[2048,768]{1,0:T(8,128)(2,1)}) %all-gather.6.cloned.1.call-update) | async-done | bytes 3145744 | tf_op jit(solution)/shard_map/all_gather | solution.py:45
  65.2 12.0 multiply_reduce_fusion
  77.3 9.1 exponential_reduce_fusion
  86.5 281.1 %all-gather.8.cloned.1.call-done = f32[262144]{0:T(1024)} async-done(((f32[2048]{0:T(1024)}), f32[262144]{0:T(1024)}) %all-gather.8.cloned.1.call-update) | async-done | bytes 1048592 | tf_op jit(solution)/shard_map/all_gather | solution.py:10
  367.6 2.4 reshape.219
  370.0 291.6 %all-gather.10.cloned.1.call-done = f32[262144]{0:T(1024)} async-done(((f32[2048]{0:T(1024)}), f32[262144]{0:T(1024)}) %all-gather.10.cloned.1.call-update) | async-done | bytes 1048592 | tf_op jit(solution)/shard_map/all_gather | solution.py:10
  662.3 2.4 reshape.220
  664.7 118.6 %while.17 = (s32[]{:T(128)}, f32[2048]{0:T(1024)S(1)}, f32[2048]{0:T(1024)S(1)}, f32[128,2048]{1,0:T(8,128)}, f32[128,2048]{1,0:T(8,128)}, /*index=5*/s32[]{:T(128)}, s32[]{:T(128)}, s32[]{:T(128)}) while((s32[]{:T(128)}, f32[2048]{0:T(1024)S(1)}, f32[2048]{0:T(1024)S(1)}, f32[128,2048]{1,0:T(8,128)}, f32[128,2048]{1,0:T(8,128)}, ...), condition=%wide.region_3.4_spmd, body=%wide.region_2.3_spmd.sunk | while | flops 12293 | bytes 82051 | solution.py:15
  783.3 12.3 convolution_multiply_fusion
  797.9 2.9 scatter_custom_fusion
  800.9 18.8 %all_to_all.19 = s32[128,1,8]{2,1,0:T(1,128)S(1)} all-to-all(s32[128,1,8]{2,1,0:T(1,128)S(1)} %bitcast.48), channel_id=1, replica_groups=mesh['dp'=16,'label'=8] {'dp','label'}, dimensions={0} | all-to-all | bytes 8192 | tf_op jit(solution)/shard_map/all_to_all | solution.py:77
  820.7 5.2 gather_fusion
  825.9 2.8 bitcast_select_fusion
  828.7 5.7 all-to-all-start.1
  836.3 2.4 mul.136
  838.7 20.3 %all-to-all-done.1 = bf16[128,8,768]{2,1,0:T(8,128)(2,1)} async-done(((bf16[128,8,768]{2,1,0:T(8,128)(2,1)}), bf16[128,8,768]{2,1,0:T(8,128)(2,1)}, u32[]{:S(2)}, u32[]{:S(2)}) %all-to-all-start.1) | async-done | bytes 1572896 | tf_op jit(solution)/shard_map/all_to_all | solution.py:81
  859.0 4.5 gather_fusion.1
  863.6 2.0 gather.15
  867.6 4.0 scatter_custom_fusion.1
  871.6 6.8 all-to-all-start.2
  880.0 13.2 convolution_multiply_fusion.1
  893.3 26.9 %all-to-all-done.2 = f32[128,8,768]{2,1,0:T(8,128)} async-done(((f32[128,8,768]{2,1,0:T(8,128)}), f32[128,8,768]{2,1,0:T(8,128)}, u32[]{:S(2)}, u32[]{:S(2)}) %all-to-all-start.2) | async-done | bytes 3145760 | tf_op jit(solution)/shard_map/all_to_all | solution.py:104
  920.2 13.6 scatter_custom_fusion.2
  934.4 525.8 %reduce-scatter.2.cloned.1.call-done = f32[16,768]{1,0:T(8,128)} async-done(((f32[2048,768]{1,0:T(8,128)}), f32[16,768]{1,0:T(8,128)}) %reduce-scatter.2.cloned.1.call-update) | async-done | bytes 49168 | tf_op jit(solution)/shard_map/reduce_scatter | solution.py:110
  (311 shorter events, 127.3 us)
Async XLA Ops:
  7.2 58.0 %copy-start = (bf16[2048,768]{1,0:T(8,128)(2,1)S(1)}, bf16[2048,768]{1,0:T(8,128)(2,1)}, u32[]{:S(2)}) copy-start(bf16[2048,768]{1,0:T(8,128)(2,1)} %param.7) | copy-start | bytes 9437188
  7.2 58.0 %all-gather.6.cloned.1.call-start = ((), (), s32[]{:S(2)}) async-start(), calls=%async_computation.4 | async-start | bytes 3342336 | tf_op jit(solution)/shard_map/all_gather | solution.py:45
  7.9 359.7 %all-gather.8.cloned.1.call-start = ((), (), s32[]{:S(2)}) async-start(), calls=%async_computation.6 | async-start | bytes 1056768 | tf_op jit(solution)/shard_map/all_gather | solution.py:10
  77.2 584.4 %all-gather.10.cloned.1.call-start = ((), (), s32[]{:S(2)}) async-start(), calls=%async_computation.7 | async-start | bytes 1056768 | tf_op jit(solution)/shard_map/all_gather | solution.py:10
  86.4 1373.8 %reduce-scatter.2.cloned.1.call-start = ((), (), s32[]{:S(2)}) async-start(), calls=%async_computation.5 | async-start | bytes 6340608 | tf_op jit(solution)/shard_map/reduce_scatter | solution.py:110
  367.6 297.1 %slice-start = ((f32[262144]{0:T(1024)}), f32[2048]{0:T(1024)S(1)}, s32[]{:S(2)}) async-start(f32[262144]{0:T(1024)} %all-gather.8.cloned.1.call-done), calls=%async_computation.8 | async-start | bytes 16384 | tf_op jit(solution)/shard_map/jit(dynamic_index_in_dim)/dynamic_slice | solution.py:13
  795.6 0.7 copy-start.2
  795.6 2.0 copy-start.1
  828.7 30.3 %all-to-all-start.1 = ((bf16[128,8,768]{2,1,0:T(8,128)(2,1)}), bf16[128,8,768]{2,1,0:T(8,128)(2,1)}, u32[]{:S(2)}, u32[]{:S(2)}) async-start(bf16[128,8,768]{2,1,0:T(8,128)(2,1)} %bitcast_select_fusion), calls=%async_computation.1 | async-start | bytes 3145728 | tf_op jit(solution)/shard_map/all_to_all | solution.py:81
  871.6 48.7 %all-to-all-start.2 = ((f32[128,8,768]{2,1,0:T(8,128)}), f32[128,8,768]{2,1,0:T(8,128)}, u32[]{:S(2)}, u32[]{:S(2)}) async-start(f32[128,8,768]{2,1,0:T(8,128)} %bitcast.41), calls=%async_computation.3 | async-start | bytes 6291456 | tf_op jit(solution)/shard_map/all_to_all | solution.py:104
Sparse Core Ops, SparseCore 0:
  10.4 54.6 all-gather.5
  77.3 290.2 all-gather.7
  369.3 292.2 all-gather.9
  795.7 664.4 reduce-scatter.1
where the time goes:
time: 1480 us; the launch traced here: 1470 us
  waiting for transfers between devices  1200 us (81%)
  local copies, waits for them, and re-layouts  138 us (9%)
  matrix products  39 us (3%)
  other arithmetic  38 us (3%)
  blocking collectives  18.8 us (1%)
    all_gather x2, waiting for transfers between devices, merged(): gathered = jax.tree.map(lambda a: lax.all_gather(a, axis), part)  573 us
    reduce_scatter x1, waiting for transfers between devices, shards(): lax.psum_scatter(doc_part, ('dp', 'label'), scatter_dimension=0, tiled=True)  526 us
    dynamic_slice x130, local copies, waits for them, and re-layouts, take(): lax.dynamic_index_in_dim(a, source, 0, False)  114 us
    all_gather x1, waiting for transfers between devices, shards(): lax.all_gather(documents, 'dp', axis=0, tiled=True)  57.2 us
  transfers between devices with their start and end apart: 6, of which 6 were waited for; matrix products, arithmetic and copies ran while one was open for 5% of the time, Pallas kernels for 0%

commit v1 on v0

v1 whole, which is shorter than its diff:
```python
import functools
import math

import jax
import jax.numpy as jnp
from jax import lax
from jax.experimental import pallas as pl
from jax.experimental.pallas import tpu as pltpu
from jax.sharding import PartitionSpec as P

MESH = pl.DeviceIdType.MESH
F32 = jnp.float32
BF16 = jnp.bfloat16

NX, NYH, NC, NZ, NYL = 4, 2, 2, 4, 2
DP, LB = 16, 8
DEV = DP * LB
SUB = 16
BLK = SUB * LB
GRP = 2 * BLK
DOCS = DP * BLK
D = 768
ROWS = 2048
COLS = 17
TW = 384
MSG = TW + 128
SLOTS = 8
BIG = float(2 ** 23)
FG = 256
C = 4.0 / math.sqrt(D)
TILE = 512

NT = (((1,), (1,)), ((), ()))


def mm(a, b):
    return jnp.dot(a, b, preferred_element_type=F32)


def split(v):
    hi = v.astype(BF16)
    return hi, (v - hi.astype(F32)).astype(BF16)


def kernel(
    docs_ref, labels_ref, ids_ref,
    lg_ref, dg_ref, loss_ref, logt_ref,
    dall, labt, e_ref, u_ref, rc_ref, w_ref, r1_ref, v1_ref, r2_ref, v2_ref, r3_ref,
    idl_ref, idg_ref, keys_ref, rowt_ref, lrow_ref, grow_ref, ch_ref, cl_ref,
    ts_ref, tr_ref, ss_ref, sr_ref, ca_ref, scale_ref, stage_ref,
    own_sem, doc_send, doc_recv, fwd_send, sib_send, sib_recv,
    idl_send, idl_recv, idg_send, idg_recv,
    t1_send, t1_recv, t2_send, t2_recv, t3_send, t3_recv,
    rc_send, rc_recv, rs_send, rs_recv, out_sem,
):
    dp = lax.axis_index("dp")
    lb = lax.axis_index("label")
    x, yh, co = dp // 4, (dp // 2) % 2, dp % 2
    z, yl = lb // 2, lb % 2
    y = yh * 2 + yl
    me = dp * LB + lb

    def dev(x_, yh_, co_, z_, yl_):
        return ((x_ * 2 + yh_) * 2 + co_, z_ * 2 + yl_)

    sib = dev(x, yh, 1 - co, z, yl)
    ypart = dev(x, 1 - yh, co, z, 1 - yl)

    def on_axis(axis, pos):
        if axis == 0:
            return dev(pos, yh, co, z, yl)
        if axis == 1:
            return dev(x, pos // 2, co, z, pos % 2)
        return dev(x, yh, co, pos, yl)

    def remote(src, dst, ssem, rsem, to):
        return pltpu.make_async_remote_copy(
            src_ref=src, dst_ref=dst, send_sem=ssem, recv_sem=rsem, device_id=to, device_id_type=MESH
        )

    barrier = pltpu.get_barrier_semaphore()

    def greet_dp(i, _):
        pl.semaphore_signal(barrier, inc=1, device_id=((dp + i) % DP, lb), device_id_type=MESH)
        return 0

    def greet_lb(i, _):
        pl.semaphore_signal(barrier, inc=1, device_id=(dp, (lb + i) % LB), device_id_type=MESH)
        return 0

    lax.fori_loop(1, DP, greet_dp, 0)
    lax.fori_loop(1, LB, greet_lb, 0)
    pl.semaphore_signal(barrier, inc=1, device_id=ypart, device_id_type=MESH)
    pl.semaphore_wait(barrier, DP - 1 + LB - 1 + 1)

    g_own = x * 2 + yh

    def doc_slot(group, core):
        return dall.at[group * 2 + core]

    own_copy = pltpu.make_async_copy(docs_ref, doc_slot(g_own, co), own_sem)
    own_copy.start()

    def sib_copy(k, src, group):
        return remote(src, doc_slot(group, co), sib_send.at[k], sib_recv.at[k], sib)

    sib_copy(0, docs_ref, g_own).start()
    first_sends = [
        remote(docs_ref, doc_slot(g_own, co), doc_send.at[0], doc_recv.at[1], ypart),
        remote(docs_ref, doc_slot(g_own, co), doc_send.at[1], doc_recv.at[3], on_axis(0, (x + 1) % NX)),
        remote(docs_ref, doc_slot(g_own, co), doc_send.at[2], doc_recv.at[2], on_axis(0, (x + 3) % NX)),
        remote(docs_ref, doc_slot(g_own, co), doc_send.at[3], doc_recv.at[4], on_axis(0, (x + 2) % NX)),
    ]
    for copy in first_sends:
        copy.start()

    def idl_copy(i):
        return remote(ids_ref, idl_ref.at[lb], idl_send.at[i], idl_recv.at[lb], (dp, (lb + i) % LB))

    lax.fori_loop(1, LB, lambda i, _: (idl_copy(i).start(), 0)[1], 0)

    def turn(i, _):
        r = pl.multiple_of(i * 256, 256)
        labt[:, pl.ds(r, 256)] = labels_ref[pl.ds(r, 256), :].T
        return 0

    lax.fori_loop(0, ROWS // 256, turn, 0)
    ts_ref[...] = jnp.zeros_like(ts_ref)

    def idl_sum(i, acc):
        p = (lb + i) % LB
        remote(ids_ref, idl_ref.at[p], idl_send.at[i], idl_recv.at[p], (dp, p)).wait_recv()
        return acc + idl_ref[p]

    idg_ref[dp] = lax.fori_loop(1, LB, idl_sum, ids_ref[...])

    def idg_copy(i):
        return remote(idg_ref.at[dp], idg_ref.at[dp], idg_send.at[i], idg_recv.at[dp], ((dp + i) % DP, lb))

    lax.fori_loop(1, DP, lambda i, _: (idg_copy(i).start(), 0)[1], 0)

    def place(k):
        dx = jnp.where((k == 2) | (k == 5), 1, jnp.where((k == 3) | (k == 6), 3, jnp.where((k == 4) | (k == 7), 2, 0)))
        dy = jnp.where((k == 1) | (k >= 5), 1, 0)
        return ((x + dx) % NX) * 2 + (yh + dy) % 2

    own_copy.wait()

    def score_step(k, _):
        nxt = k + 1

        @pl.when(nxt < 8)
        def _():
            g1 = place(nxt)
            slot = doc_slot(g1, co)
            remote(slot, slot, doc_send.at[0], doc_recv.at[nxt], ypart).wait_recv()
            sib_copy(nxt, slot, g1).start()

            @pl.when(nxt == 1)
            def _():
                remote(slot, slot, fwd_send.at[0], doc_recv.at[6], on_axis(0, (x + 1) % NX)).start()
                remote(slot, slot, fwd_send.at[1], doc_recv.at[5], on_axis(0, (x + 3) % NX)).start()

            @pl.when(nxt == 4)
            def _():
                remote(slot, slot, fwd_send.at[2], doc_recv.at[7], ypart).start()

        g = place(k)
        other = doc_slot(g, 1 - co)
        remote(other, other, sib_send.at[k], sib_recv.at[k], sib).wait_recv()
        block = dall[pl.ds(g * 2, 2)].reshape(GRP, D)
        s = lax.dot_general(labels_ref[...], block, NT, preferred_element_type=F32)
        top = jnp.max(s, axis=0, keepdims=True)
        e = jnp.exp((s - top) * C)
        e_ref[:, pl.ds(pl.multiple_of(g * GRP, GRP), GRP)] = e
        total = jnp.sum(e, axis=0, keepdims=True)
        top = top * C
        for h in range(2):
            ts_ref[g * 2 + h, 0:1, TW:MSG] = top[:, h * BLK:(h + 1) * BLK]
            ts_ref[g * 2 + h, 1:2, TW:MSG] = total[:, h * BLK:(h + 1) * BLK]
        return 0

    lax.fori_loop(0, 8, score_step, 0)

    lane_t = lax.broadcasted_iota(jnp.int32, (LB, TW), 1).astype(F32)
    base = (me * ROWS).astype(F32)

    def find(b, _):
        @pl.when(b != dp)
        def _():
            remote(idg_ref.at[b], idg_ref.at[b], idg_send.at[b], idg_recv.at[b], (b, lb)).wait_recv()

        rel = idg_ref[b] - base
        key = jnp.where((rel >= 0.0) & (rel < float(ROWS)), lane_t * float(ROWS) + rel, BIG)
        for k in range(SLOTS):
            low = jnp.min(key, axis=1, keepdims=True)
            keys_ref[pl.ds(pl.multiple_of((b * SLOTS + k) * 8, 8), 8), :] = jnp.broadcast_to(low, (8, 128))
            key = jnp.where(key == low, BIG, key)
        return 0

    lax.fori_loop(0, DP, find, 0)

    def parts_of(key):
        t = jnp.floor(key * (1.0 / ROWS))
        row = jnp.where(key < BIG, key - t * float(ROWS), -1.0)
        return t, row

    lane_rows = lax.broadcasted_iota(jnp.int32, (256, ROWS), 1).astype(F32)

    def fetch(i, _):
        r = pl.multiple_of(i * 256, 256)
        _, row = parts_of(keys_ref[pl.ds(r, 256), :][:, 0:1])
        pick = jnp.where(lane_rows == row, 1.0, 0.0).astype(BF16)
        lrow_ref[pl.ds(r, 256), :] = mm(pick, labels_ref[...]).astype(BF16)
        return 0

    lax.fori_loop(0, 4, fetch, 0)

    def flip(i, _):
        _, row = parts_of(keys_ref[pl.ds(pl.multiple_of(i * 128, 128), 128), :])
        rowt_ref[:, pl.ds(pl.multiple_of(i * 128, 128), 128)] = row.T[0:8, :]
        return 0

    lax.fori_loop(0, 8, flip, 0)

    lane_doc = lax.broadcasted_iota(jnp.int32, (64, BLK), 1).astype(F32)
    slot_l = (lax.broadcasted_iota(jnp.int32, (64, 1), 0) % 8).astype(F32)

    def doc_pick(key):
        t, _ = parts_of(key)
        d = t - 16.0 * jnp.floor(t * (1.0 / 16.0)) + 16.0 * slot_l
        d = jnp.where(key < BIG, d, -1.0)
        return jnp.where(lane_doc == d, 1.0, 0.0)

    def target(b, _):
        r = pl.multiple_of(b * 64, 64)
        key = keys_ref[pl.ds(r, 64), :][:, 0:1]
        t, _ = parts_of(key)
        found = mm(doc_pick(key).astype(BF16), dall[b])
        grow_ref[pl.ds(r, 64), :] = found.astype(BF16)
        score = C * jnp.sum(found * lrow_ref[pl.ds(r, 64), :].astype(F32), axis=1, keepdims=True)
        acc = jnp.zeros((LB, TW), F32)
        for k in range(SLOTS):
            acc = acc + jnp.where(lane_t == t[k * 8:k * 8 + 8], score[k * 8:k * 8 + 8], 0.0)
        ts_ref[b, :, 0:TW] = acc
        return 0

    lax.fori_loop(0, DP, target, 0)

    def t1_copy(i):
        q = (dp + i) % DP
        return remote(ts_ref.at[q], tr_ref.at[dp], t1_send.at[i], t1_recv.at[dp], (q, lb))

    lax.fori_loop(1, DP, lambda i, _: (t1_copy(i).start(), 0)[1], 0)

    def doc_mm(g, _):
        cols = pl.ds(pl.multiple_of(g * GRP, GRP), GRP)
        part = mm(labt[...], e_ref[:, cols].astype(BF16))
        u_ref[pl.ds(pl.multiple_of(g * GRP, GRP), GRP), :] = part.T
        return 0

    lax.fori_loop(0, 3, doc_mm, 0)

    tr_ref[dp] = ts_ref[dp]

    def t1_wait(i, top):
        q = (dp + i) % DP
        remote(ts_ref.at[q], tr_ref.at[q], t1_send.at[i], t1_recv.at[q], (q, lb)).wait_recv()
        return jnp.maximum(top, tr_ref[q, 0:1, TW:MSG])

    top = lax.fori_loop(1, DP, t1_wait, tr_ref[dp, 0:1, TW:MSG])

    def t1_sum(q, state):
        total, acc = state
        total = total + tr_ref[q, 1:2, TW:MSG] * jnp.exp(tr_ref[q, 0:1, TW:MSG] - top)
        return total, acc + tr_ref[q, :, 0:TW]

    total, acc = lax.fori_loop(0, DP, t1_sum, (jnp.zeros((1, BLK), F32), jnp.zeros((LB, TW), F32)))
    ss_ref[:, 0:TW] = acc
    ss_ref[:, TW:MSG] = jnp.zeros((LB, BLK), F32)
    ss_ref[0:1, TW:MSG] = top
    ss_ref[1:2, TW:MSG] = total

    def t2_copy(i):
        return remote(ss_ref, sr_ref.at[lb], t2_send.at[i], t2_recv.at[lb], (dp, (lb + i) % LB))

    lax.fori_loop(1, LB, lambda i, _: (t2_copy(i).start(), 0)[1], 0)
    lax.fori_loop(3, 6, doc_mm, 0)
    sr_ref[lb] = ss_ref[...]

    def t2_wait(i, top):
        q = (lb + i) % LB
        remote(ss_ref, sr_ref.at[q], t2_send.at[i], t2_recv.at[q], (dp, q)).wait_recv()
        return jnp.maximum(top, sr_ref[q, 0:1, TW:MSG])

    top = lax.fori_loop(1, LB, t2_wait, ss_ref[0:1, TW:MSG])

    def t2_sum(q, state):
        total, acc = state
        total = total + sr_ref[q, 1:2, TW:MSG] * jnp.exp(sr_ref[q, 0:1, TW:MSG] - top)
        return total, acc + sr_ref[q, :, 0:TW]

    total, acc = lax.fori_loop(0, LB, t2_sum, (jnp.zeros((1, BLK), F32), jnp.zeros((LB, TW), F32)))
    log_total = top + jnp.log(total)
    logt_ref[...] = jnp.broadcast_to(log_total, (8, 128))

    lane = lax.broadcasted_iota(jnp.int32, (LB, 128), 1)
    pos = jnp.where(lane < 16, acc[:, 0:128], 0.0)
    for s in (16, 32, 64):
        pos = pos + pltpu.roll(pos, s, 1)
    soft = jnp.zeros((LB, 128), F32)
    weight = jnp.zeros((LB, 128), F32)
    pieces = []
    for v in range(3):
        gap = acc[:, v * 128:(v + 1) * 128] - pos + 1.0
        use = (lane >= 16) if v == 0 else (lane >= 0) if v == 1 else (lane < 16)
        small = jnp.exp(-jnp.abs(gap))
        soft = soft + jnp.where(use, jnp.maximum(gap, 0.0) + jnp.log(1.0 + small), 0.0)
        sig = jnp.where(use, jnp.where(gap >= 0.0, 1.0, small) / (1.0 + small) * (1.0 / 16.0), 0.0)
        weight = weight + sig
        pieces.append(sig)
    for s in (16, 32, 64):
        soft = soft + pltpu.roll(soft, s, 1)
        weight = weight + pltpu.roll(weight, s, 1)
    loss_ref[...] = soft * (1.0 / 16.0) - pos
    pieces[0] = jnp.where(lane < 16, -1.0 - weight, pieces[0])
    for v in range(3):
        ca_ref[dp, :, v * 128:(v + 1) * 128] = pieces[v]
    ca_ref[dp, :, TW:MSG] = jnp.broadcast_to(log_total, (LB, BLK))

    def t3_copy(i):
        return remote(ca_ref.at[dp], ca_ref.at[dp], t3_send.at[i], t3_recv.at[dp], ((dp + i) % DP, lb))

    lax.fori_loop(1, DP, lambda i, _: (t3_copy(i).start(), 0)[1], 0)
    lax.fori_loop(6, 8, doc_mm, 0)

    def t3_wait(i, _):
        q = (dp + i) % DP
        remote(ca_ref.at[q], ca_ref.at[q], t3_send.at[i], t3_recv.at[q], (q, lb)).wait_recv()
        return 0

    lax.fori_loop(1, DP, t3_wait, 0)

    def slot_coef(b, t):
        dense = ca_ref[b, :, 0:TW]
        out = [jnp.sum(jnp.where(lane_t == t[k * 8:k * 8 + 8], dense, 0.0), axis=1, keepdims=True) for k in range(SLOTS)]
        return jnp.concatenate(out, axis=0)

    def core_copy(j):
        block = u_ref.at[pl.ds(pl.multiple_of((j * 2 + 1 - co) * BLK, BLK), BLK), :]
        return remote(block, rc_ref.at[j], rc_send.at[j], rc_recv.at[j], sib)

    def finish(i, _):
        j = i % 8
        b = j * 2 + jnp.where(i < 8, 1 - co, co)
        r = pl.multiple_of(b * 64, 64)
        key = keys_ref[pl.ds(r, 64), :][:, 0:1]
        t, _ = parts_of(key)
        coef = slot_coef(b, t)
        keys_ref[pl.ds(r, 64), 64:128] = jnp.broadcast_to(coef, (64, 64))
        hi, lo = split(coef * lrow_ref[pl.ds(r, 64), :].astype(F32))
        pick = doc_pick(key)
        pick = jnp.concatenate([pick, pick], axis=0).T.astype(BF16)
        hard = mm(pick, jnp.concatenate([hi, lo], axis=0))
        scale = jnp.exp(ts_ref[b, 0:1, TW:MSG] - ca_ref[b, 0:1, TW:MSG])
        scale_ref[:, pl.ds(pl.multiple_of(b * BLK, BLK), BLK)] = jnp.broadcast_to(scale, (8, BLK))
        col = jnp.broadcast_to(scale, (BLK, BLK)).T[:, 0:1]
        rows = pl.ds(pl.multiple_of(b * BLK, BLK), BLK)
        u_ref[rows, :] = C * (u_ref[rows, :] * col + hard)

        @pl.when(i < 8)
        def _():
            core_copy(j).start()

        return 0

    lax.fori_loop(0, 16, finish, 0)

    def gather_units(j, _):
        core_copy(j).wait_recv()
        xx, hh = j // 2, j % 2
        for zz in range(NZ):
            for ll in range(NYL):
                off = (zz * NYL + ll) * SUB
                rows = pl.ds(pl.multiple_of((j * 2 + co) * BLK + off, SUB), SUB)
                u = u_ref[rows, :] + rc_ref[j, off:off + SUB, :]
                yy = hh * 2 + ll
                w_ref[0, xx, yy, zz] = u[:, 0:FG]
                w_ref[1, yy, zz, xx] = u[:, FG:2 * FG]
                w_ref[2, zz, xx, yy] = u[:, 2 * FG:3 * FG]
        return 0

    lax.fori_loop(0, 8, gather_units, 0)

    spot = (x, y, z)
    bufs = ((w_ref, r1_ref), (v1_ref, r2_ref), (v2_ref, r3_ref))

    def rs_copy(step, f, i):
        axis = (f + step) % 3
        here = spot[axis]
        to = (here + i) % 4
        src, dst = bufs[step]
        n = (step * 3 + f) * 4
        return remote(src.at[f, to], dst.at[f, here], rs_send.at[n + i], rs_recv.at[n + here], on_axis(axis, to))

    def rs_wait(step, f, i):
        axis = (f + step) % 3
        frm = (spot[axis] + i) % 4
        src, dst = bufs[step]
        n = (step * 3 + f) * 4
        remote(src.at[f, frm], dst.at[f, frm], rs_send.at[n + i], rs_recv.at[n + frm], on_axis(axis, frm)).wait_recv()

    def rs_start(step):
        for f in range(3):
            for i in (2, 1, 3):
                rs_copy(step, f, i).start()

    def rs_sum(step, f):
        src, dst = bufs[step]
        here = spot[(f + step) % 3]
        for i in (1, 3, 2):
            rs_wait(step, f, i)
        value = src[f, here]
        for i in (1, 2, 3):
            value = value + dst[f, (here + i) % 4]
        return value

    rs_start(0)

    def hard_rows(i, _):
        r = pl.multiple_of(i * 64, 64)
        coef = keys_ref[pl.ds(r, 64), :][:, 64:65]
        hi, lo = split(coef * grow_ref[pl.ds(r, 64), :].astype(F32))
        ch_ref[pl.ds(r, 64), :] = hi
        cl_ref[pl.ds(r, 64), :] = lo
        return 0

    lax.fori_loop(0, 16, hard_rows, 0)

    def out_copy(i):
        return pltpu.make_async_copy(
            stage_ref.at[i % 2], lg_ref.at[pl.ds(pl.multiple_of(i * TILE, TILE), TILE), :], out_sem.at[i]
        )

    def label_mm(i, _):
        r = pl.multiple_of(i * TILE, TILE)
        probs = (e_ref[pl.ds(r, TILE), :] * scale_ref[0:1, :]).astype(BF16)
        value = mm(probs, dall[...].reshape(DOCS, D))
        sub_rows = (lax.broadcasted_iota(jnp.int32, (TILE, DEV * SLOTS), 0) + r).astype(F32)
        pick = jnp.where(sub_rows == rowt_ref[0:1, :], 1.0, 0.0).astype(BF16)
        value = value + mm(pick, ch_ref[...]) + mm(pick, cl_ref[...])

        @pl.when(i >= 2)
        def _():
            out_copy(i - 2).wait()

        stage_ref[i % 2] = C * value
        out_copy(i).start()
        return 0

    lax.fori_loop(0, 2, label_mm, 0)
    for f in range(3):
        v1_ref[f] = rs_sum(0, f)
    rs_start(1)
    lax.fori_loop(2, 3, label_mm, 0)
    for f in range(3):
        v2_ref[f] = rs_sum(1, f)
    rs_start(2)
    lax.fori_loop(3, 4, label_mm, 0)
    for f in range(3):
        dg_ref[:, f * FG:(f + 1) * FG] = rs_sum(2, f)

    out_copy(2).wait()
    out_copy(3).wait()
    for copy in first_sends:
        copy.wait_send()
    for n in range(2):
        remote(docs_ref, doc_slot(g_own, co), fwd_send.at[n], doc_recv.at[5], ypart).wait_send()
    remote(docs_ref, doc_slot(g_own, co), fwd_send.at[2], doc_recv.at[7], ypart).wait_send()

    def ends8(k, _):
        sib_copy(k, docs_ref, g_own).wait_send()
        core_copy(k).wait_send()
        return 0

    lax.fori_loop(0, 8, ends8, 0)

    def ends_lb(i, _):
        idl_copy(i).wait_send()
        t2_copy(i).wait_send()
        return 0

    lax.fori_loop(1, LB, ends_lb, 0)

    def ends_dp(i, _):
        idg_copy(i).wait_send()
        t1_copy(i).wait_send()
        t3_copy(i).wait_send()
        return 0

    lax.fori_loop(1, DP, ends_dp, 0)
    for step in range(3):
        for f in range(3):
            for i in (1, 2, 3):
                rs_copy(step, f, i).wait_send()


def shards(documents, labels, target_owner, target_row):
    lb = lax.axis_index("label")
    ids = (target_owner[:, :, 0] * ROWS + target_row).T.reshape(1, SUB * COLS).astype(F32)
    ids = jnp.pad(ids, ((0, 0), (0, TW - SUB * COLS)), constant_values=-1.0)
    ids = jnp.where(lax.broadcasted_iota(jnp.int32, (LB, TW), 0) == lb, ids, 0.0)
    vm = pl.BlockSpec(memory_space=pltpu.VMEM)
    dma = pltpu.SemaphoreType.DMA
    label_grad, doc_grad, loss, logt = pl.pallas_call(
        kernel,
        out_shape=(
            jax.ShapeDtypeStruct((ROWS, D), F32),
            jax.ShapeDtypeStruct((SUB, D), F32),
            jax.ShapeDtypeStruct((8, 128), F32),
            jax.ShapeDtypeStruct((8, 128), F32),
        ),
        in_specs=[vm, vm, vm],
        out_specs=(pl.BlockSpec(memory_space=pl.ANY), vm, vm, vm),
        scratch_shapes=[
            pltpu.VMEM((DP, BLK, D), BF16),
            pltpu.VMEM((D, ROWS), BF16),
            pltpu.VMEM((ROWS, DOCS), F32),
            pltpu.VMEM((DOCS, D), F32),
            pltpu.VMEM((8, BLK, D), F32),
            pltpu.VMEM((3, 4, 4, 4, SUB, FG), F32),
            pltpu.VMEM((3, 4, 4, 4, SUB, FG), F32),
            pltpu.VMEM((3, 4, 4, SUB, FG), F32),
            pltpu.VMEM((3, 4, 4, SUB, FG), F32),
            pltpu.VMEM((3, 4, SUB, FG), F32),
            pltpu.VMEM((3, 4, SUB, FG), F32),
            pltpu.VMEM((LB, LB, TW), F32),
            pltpu.VMEM((DP, LB, TW), F32),
            pltpu.VMEM((DEV * SLOTS, 128), F32),
            pltpu.VMEM((8, DEV * SLOTS), F32),
            pltpu.VMEM((DEV * SLOTS, D), BF16),
            pltpu.VMEM((DEV * SLOTS, D), BF16),
            pltpu.VMEM((DEV * SLOTS, D), BF16),
            pltpu.VMEM((DEV * SLOTS, D), BF16),
            pltpu.VMEM((DP, LB, MSG), F32),
            pltpu.VMEM((DP, LB, MSG), F32),
            pltpu.VMEM((LB, MSG), F32),
            pltpu.VMEM((LB, LB, MSG), F32),
            pltpu.VMEM((DP, LB, MSG), F32),
            pltpu.VMEM((8, DOCS), F32),
            pltpu.VMEM((2, TILE, D), F32),
            dma,
            dma((4,)), dma((8,)), dma((3,)), dma((8,)), dma((8,)),
            dma((LB,)), dma((LB,)), dma((DP,)), dma((DP,)),
            dma((DP,)), dma((DP,)), dma((LB,)), dma((LB,)), dma((DP,)), dma((DP,)),
            dma((8,)), dma((8,)), dma((36,)), dma((36,)), dma((4,)),
        ],
        compiler_params=pltpu.CompilerParams(
            collective_id=0, has_side_effects=True, vmem_limit_bytes=62 * 1024 * 1024
        ),
        cost_estimate=pl.CostEstimate(
            flops=8 * ROWS * DOCS * D, bytes_accessed=10 * ROWS * D, transcendentals=ROWS * DOCS
        ),
        name="head",
    )(documents, labels, ids)
    doc_loss = (
        lax.dynamic_slice(loss, (lb, 0), (1, SUB)) + lax.dynamic_slice(logt, (0, lb * SUB), (1, SUB))
    ).reshape(SUB)
    return doc_loss, doc_grad, label_grad


def solution(mesh):
    return jax.shard_map(
        shards,
        mesh=mesh,
        in_specs=(
            P("dp", None),
            P(("dp", "label"), None),
            P(("dp", "label"), None, None),
            P(("dp", "label"), None),
        ),
        out_specs=(P(("dp", "label")), P(("dp", "label"), None), P(("dp", "label"), None)),
        check_vma=False,
    )
```

time: 1480 us -> 124 us (0.08)
  waiting for transfers between devices: 1200 us -> 0 us
  local copies, waits for them, and re-layouts: 138 us -> 7.51 us
  Pallas kernels: 0 us -> 111 us
  matrix products: 39 us -> 0 us
  other arithmetic: 38 us -> 2.68 us
  blocking collectives: 18.8 us -> 0 us
    all_gather x3 -> x0, waiting for transfers between devices: 630 us -> none  [the longest x2 573 us: merged(): gathered = jax.tree.map(lambda a: lax.all_gather(a, axis), part)]
    reduce_scatter x1 -> x0, waiting for transfers between devices: 526 us -> none  [shards(): lax.psum_scatter(doc_part, ('dp', 'label'), scatter_dimension=0, tiled=True)]
    dynamic_slice x130 -> x0, local copies, waits for them, and re-layouts: 114 us -> none  [take(): lax.dynamic_index_in_dim(a, source, 0, False)]
    pallas_call x0 -> x1, Pallas kernels: none -> 111 us  [shards(): pl.pallas_call(kernel, out_shape=(jax.ShapeDtypeStruct((ROWS, D), F32), j...]
    all_to_all x2 -> x0, waiting for transfers between devices: 47.3 us -> none  [the longest x1 26.9 us: shards(): lax.all_to_all(send_grads, ('dp', 'label'), split_axis=0, concat_axis=0,...]
    dot_general x4 -> x0, matrix products: 39 us -> none  [the longest x1 13.2 us: shards(): lax.dot_general(probabilities, doc_piece, (((0,), (0,)), ((), ())), prefe...]
    all_to_all x1 -> x0, blocking collectives: 18.8 us -> none  [shards(): lax.all_to_all(send_rows, ('dp', 'label'), split_axis=0, concat_axis=0, t...]
  transfers between devices with their start and end apart: 6 -> 0, of which waited for: 6 -> 0; matrix products, arithmetic and copies ran while one was open for 5% -> 0% of each run, Pallas kernels for 0% -> 0%
where the time goes in v1:
time: 124 us; the launch traced here: 122 us
  Pallas kernels  111 us (90%)
  local copies, waits for them, and re-layouts  7.51 us (6%)
  other arithmetic  2.68 us (2%)
    pallas_call x1, Pallas kernels, shards(): pl.pallas_call(kernel, out_shape=(jax.ShapeDtypeStruct((ROWS, D), F32), j...  111 us
    unnamed x2, local copies, waits for them, and re-layouts  7.31 us

profile of v1, /device:TPU:0, one launch (start us, length us, event | category | flops | bytes accessed | tf_op | source)
XLA Modules:
  0.0 122.3 jit_solution(5970254807501652101)
XLA Ops:
  0.6 0.7 fusion.1
  1.4 0.1 copy.9
  1.5 0.1 convert_element_type.19
  1.6 0.7 broadcast_select_fusion.ids_ref
  2.2 111.5 %head.1 = (f32[2048,768]{1,0:T(8,128)}, f32[16,768]{1,0:T(8,128)}, f32[8,128]{1,0:T(8,128)}, f32[8,128]{1,0:T(8,128)}) custom-call(bf16[128,768]{1,0:T(8,128)(2,1)} %docs_ref.1, bf16[2048,768]{1,0:T(8,128)(2,1)} %labels_ref.1, f32[8,384]{1,0:T(8,128)} %broadcast_select_fusion.ids_ref), custom_call_target="tpu_custom_call" | custom-call | flops 25769803776 | bytes 15728640 | tf_op jit(solution)/shard_map/head/pallas_call | solution.py:515
  113.7 1.3 %add_bitcast_fusion = f32[16]{0:T(128)} fusion(f32[8,128]{1,0:T(8,128)} %get-tuple-element.8, s32[]{:T(128)S(6)} %select_n.12, f32[8,128]{1,0:T(8,128)} %get-tuple-element.7, s32[]{:T(128)S(6)} %select_n.11), kind=kLoop, calls=%fused_computation.5 | loop fusion | flops 16 | bytes 200 | tf_op jit(solution)/shard_map/reshape | solution.py:568
  115.0 1.4 %copy.12 = f32[16,768]{1,0:T(8,128)} copy(f32[16,768]{1,0:T(8,128)} %get-tuple-element.15) | data formatting | bytes 98304
  116.4 5.9 %copy.13 = f32[2048,768]{1,0:T(8,128)} copy(f32[2048,768]{1,0:T(8,128)} %get-tuple-element.16) | data formatting | bytes 12582912
  (2 shorter events, 0.0 us)

commit v2 on v0

v2 whole, which is shorter than its diff:
```python
import functools
import math

import jax
import jax.numpy as jnp
from jax import lax
from jax.experimental import pallas as pl
from jax.experimental.pallas import tpu as pltpu
from jax.sharding import PartitionSpec as P

MESH = pl.DeviceIdType.MESH
F32 = jnp.float32
BF16 = jnp.bfloat16

NX, NYH, NC, NZ, NYL = 4, 2, 2, 4, 2
DP, LB = 16, 8
DEV = DP * LB
SUB = 16
BLK = SUB * LB
GRP = 2 * BLK
DOCS = DP * BLK
D = 768
ROWS = 2048
COLS = 17
TW = 384
SLOTS = 8
BIG = float(2 ** 23)
FG = 256
C = 4.0 / math.sqrt(D)
TILE = 256

NT = (((1,), (1,)), ((), ()))


def mm(a, b):
    return jnp.dot(a, b, preferred_element_type=F32)


def split(v):
    hi = v.astype(BF16).astype(F32)
    return hi, v - hi


def kernel(
    docs_ref, labels_hbm, owner_ref, row_ref,
    lg_ref, dg_ref, loss_ref,
    lab, dall, labt, e_ref, u_ref, rc_ref, w_ref, v1_ref, v2_ref, q0_ref, q1_ref, q2_ref,
    ids_ref, idl_ref, idg_ref, keys_ref, skeys_ref, rowt_ref, lrow_ref, slr_ref, grow_ref,
    st_ref, sr_ref, sv_ref, sst_ref, lt_ref,
    ts_ref, tr_ref, tu_ref, tv_ref, ca_ref, scale_ref, tmp_ref, coef_ref, coeft_ref,
    lab_sem, own_sem, doc_send, doc_recv, sib_send, sib_recv,
    idl_send, idl_recv, idg_send, idg_recv,
    s1_send, s1_recv, s2_send, s2_recv, sst_sem, lr_sem,
    t1_send, t1_recv, t2_send, t2_recv, t3_send, t3_recv,
    rc_send, rc_recv, rs_send, rs_recv,
):
    dp = lax.axis_index("dp")
    lb = lax.axis_index("label")
    x, yh, co = dp // 4, (dp // 2) % 2, dp % 2
    z, yl = lb // 2, lb % 2
    y = yh * 2 + yl
    me = dp * LB + lb

    def dev(x_, yh_, co_, z_, yl_):
        return ((x_ * 2 + yh_) * 2 + co_, z_ * 2 + yl_)

    sib = dev(x, yh, 1 - co, z, yl)
    ypart = dev(x, 1 - yh, co, z, 1 - yl)

    def on_axis(axis, pos):
        if axis == 0:
            return dev(pos, yh, co, z, yl)
        if axis == 1:
            return dev(x, pos // 2, co, z, pos % 2)
        return dev(x, yh, co, pos, yl)

    xup, xdown = on_axis(0, (x + 1) % NX), on_axis(0, (x + 3) % NX)

    def mate(i):
        q = (dp + i) % DP
        return q, (q, z * 2 + jnp.where((q // 2) % 2 == yh, yl, 1 - yl))

    def all_in(ref, sem):
        pltpu.make_async_remote_copy(
            src_ref=ref, dst_ref=ref, send_sem=sem, recv_sem=sem, device_id=sib, device_id_type=MESH
        ).wait_recv()

    def all_out(ref, sem):
        pltpu.make_async_remote_copy(
            src_ref=ref, dst_ref=ref, send_sem=sem, recv_sem=sem, device_id=sib, device_id_type=MESH
        ).wait_send()

    def remote(src, dst, ssem, rsem, to):
        return pltpu.make_async_remote_copy(
            src_ref=src, dst_ref=dst, send_sem=ssem, recv_sem=rsem, device_id=to, device_id_type=MESH
        )

    def each(lo, hi, fn):
        def body(i, carry):
            fn(i)
            return carry

        lax.fori_loop(lo, hi, body, 0)

    def at(start, size):
        return pl.ds(pl.multiple_of(start, size), size)

    barrier = pltpu.get_barrier_semaphore()
    each(1, DP, lambda i: pl.semaphore_signal(barrier, inc=1, device_id=mate(i)[1], device_id_type=MESH))
    each(1, LB, lambda i: pl.semaphore_signal(barrier, inc=1, device_id=(dp, (lb + i) % LB), device_id_type=MESH))
    pl.semaphore_signal(barrier, inc=1, device_id=dev(x, 1 - yh, co, z, yl), device_id_type=MESH)
    lab_copy = pltpu.make_async_copy(labels_hbm, lab, lab_sem)
    lab_copy.start()
    g_own = x * 2 + yh

    def doc_slot(group, core):
        return dall.at[group * 2 + core]

    own_copy = pltpu.make_async_copy(docs_ref, doc_slot(g_own, co), own_sem)
    own_copy.start()
    named = (owner_ref[:, 0, :] * ROWS + row_ref[...]).astype(F32)
    high = jnp.floor(named * (1.0 / 4096.0))
    rest = named - 4096.0 * high
    mid = jnp.floor(rest * (1.0 / 64.0))
    digits = jnp.concatenate([high, mid, rest - 64.0 * mid], axis=0).astype(BF16)
    lane = lax.broadcasted_iota(jnp.int32, (COLS, TW), 1)
    spread = mm(digits, jnp.where(lane // SUB == lax.broadcasted_iota(jnp.int32, (COLS, TW), 0), 1.0, 0.0).astype(BF16))
    spread = 4096.0 * spread[0:SUB] + 64.0 * spread[SUB:2 * SUB] + spread[2 * SUB:3 * SUB]
    lane = lax.broadcasted_iota(jnp.int32, (SUB, TW), 1)
    own = jnp.sum(jnp.where(lane % SUB == lax.broadcasted_iota(jnp.int32, (SUB, TW), 0), spread, 0.0), axis=0, keepdims=True)
    own = jnp.where(lane[0:1] < SUB * COLS, own, -1.0)
    ids_ref[...] = jnp.where(lax.broadcasted_iota(jnp.int32, (LB, TW), 0) == lb, own, 0.0)
    pl.semaphore_wait(barrier, DP - 1 + LB - 1 + 1)

    def idl_copy(i):
        return remote(ids_ref, idl_ref.at[lb], idl_send, idl_recv, (dp, (lb + i) % LB))

    each(1, LB, lambda i: idl_copy(i).start())

    def sib_copy(k, src, group):
        return remote(src, doc_slot(group, co), sib_send, sib_recv.at[k], sib)

    sib_copy(0, docs_ref, g_own).start()
    first_sends = [
        remote(docs_ref, doc_slot(g_own, co), doc_send, doc_recv.at[1], ypart),
        remote(docs_ref, doc_slot(g_own, co), doc_send, doc_recv.at[3], xup),
        remote(docs_ref, doc_slot(g_own, co), doc_send, doc_recv.at[2], xdown),
    ]
    for copy in first_sends:
        copy.start()

    def place(k):
        dx = jnp.where((k == 2) | (k == 5), 1, jnp.where((k == 3) | (k == 6), 3, jnp.where((k == 4) | (k == 7), 2, 0)))
        dy = jnp.where((k == 1) | (k >= 5), 1, 0)
        return ((x + dx) % NX) * 2 + (yh + dy) % 2

    def half(ref, h):
        return ref.at[h * (BLK // 2):(h + 1) * (BLK // 2), :]

    def relay_up(slot):
        return remote(slot, slot, doc_send, doc_recv.at[6], xup)

    def relay_down(slot):
        return remote(slot, slot, doc_send, doc_recv.at[5], xdown)

    def relay_far_a(slot):
        return remote(half(slot, 0), half(slot, 0), doc_send, doc_recv.at[4], xdown)

    def relay_far_b(slot):
        return remote(half(slot, 1), half(slot, 1), doc_send, doc_recv.at[8], xup)

    def relay_y(slot):
        return remote(slot, slot, doc_send, doc_recv.at[7], ypart)

    def take(k):
        slot = doc_slot(place(k), co)

        if k != 4:
            remote(slot, slot, doc_send, doc_recv.at[k], ypart).wait_recv()
        else:
            for h in range(2):
                remote(half(slot, h), half(slot, h), doc_send, doc_recv.at[4 + 4 * h], ypart).wait_recv()

        if k == 2:
            relay_far_a(slot).start()
        if k == 3:
            relay_far_b(slot).start()
        if k == 4:
            relay_y(slot).start()
        sib_copy(k, slot, place(k)).start()

    ts_ref[...] = jnp.zeros_like(ts_ref)
    st_ref[...] = jnp.zeros_like(st_ref)
    lab_copy.wait()

    def turn(i):
        labt[:, at(i * 256, 256)] = lab[at(i * 256, 256), :].T

    each(0, ROWS // 256, turn)

    own_copy.wait()

    def raw_cols(p):
        return slice(p * GRP, (p + 1) * GRP)

    CH = 512

    def exp_rows(p, c, top, cols):
        s = lg_ref[c * CH:(c + 1) * CH, raw_cols(p)]
        e = jnp.exp((s - top) * C)
        e_ref[c * CH:(c + 1) * CH, cols] = e
        return jnp.sum(e, axis=0, keepdims=True)

    def keep(g, top, total):
        for h in range(2):
            st_ref[0, pl.ds(g * 2 + h, 1), :] = (top * C)[:, h * BLK:(h + 1) * BLK]
            st_ref[1, pl.ds(g * 2 + h, 1), :] = total[:, h * BLK:(h + 1) * BLK]

    def wait_sib(k):
        other = doc_slot(place(k), 1 - co)
        remote(other, other, sib_send, sib_recv.at[k], sib).wait_recv()

    def score_step(k, p, old_top):
        g = place(k)

        @pl.when(k < 7)
        def _():
            wait_sib(k)

        block = dall[pl.ds(g * 2, 2)].reshape(GRP, D)
        old = place((k + 7) % 8)
        cols = at(old * GRP, GRP)
        top, total = None, 0.0
        for c in range(ROWS // CH):
            s = lax.dot_general(lab[c * CH:(c + 1) * CH, :], block, NT, preferred_element_type=F32)
            lg_ref[c * CH:(c + 1) * CH, raw_cols(p)] = s
            high = jnp.max(s, axis=0, keepdims=True)
            top = high if top is None else jnp.maximum(top, high)
            total = total + exp_rows(1 - p, c, old_top, cols)
        keep(old, old_top, total)
        return top

    def ids_out():
        all_in(idl_ref.at[1:LB], idl_recv)
        idl_ref[lb] = ids_ref[...]
        acc = idl_ref[0]
        for q in range(1, LB):
            acc = acc + idl_ref[q]
        idg_ref[dp] = acc
        each(1, DP, lambda i: idg_copy(i).start())

    def idg_copy(i):
        return remote(idg_ref.at[dp], idg_ref.at[dp], idg_send, idg_recv, mate(i)[1])

    lane_8 = lax.broadcasted_iota(jnp.int32, (LB, 128), 1).astype(F32)
    lane_t = [lane_8 + 128.0 * v for v in range(3)]
    base = (me * ROWS).astype(F32)

    def find():
        all_in(idg_ref.at[1:DP], idg_recv)
        rel = idg_ref[...].reshape(DEV, TW) - base
        lanes = lax.broadcasted_iota(jnp.int32, (DEV, TW), 1).astype(F32)
        key = jnp.where((rel >= 0.0) & (rel < float(ROWS)), lanes * float(ROWS) + rel, BIG)
        for k in range(SLOTS):
            low = jnp.min(key, axis=1, keepdims=True)
            for b in range(DP):
                keys_ref[b % 2, b // 2, k * 8:k * 8 + 8, :] = jnp.broadcast_to(low[b * 8:b * 8 + 8], (8, 128))
            key = jnp.where(key == low, BIG, key)

    def parts_of(key):
        t = jnp.floor(key * (1.0 / ROWS))
        row = jnp.where(key < BIG, key - t * float(ROWS), -1.0)
        return t, row

    def fetch(i):
        lane_rows = lax.broadcasted_iota(jnp.int32, (256, ROWS), 1).astype(F32)
        c, j = i // 2, pl.ds((i % 2) * 4, 4)
        _, row = parts_of(keys_ref[c, j].reshape(256, 128)[:, 0:1])
        pick = jnp.where(lane_rows == row, 1.0, 0.0).astype(BF16)
        lrow_ref[c, j] = mm(pick, lab[...]).astype(BF16).reshape(4, 64, D)

    def named_copy():
        return remote(lrow_ref.at[1 - co], slr_ref, lr_sem.at[0], lr_sem.at[1], sib)

    def keys_copy():
        return remote(keys_ref.at[1 - co], skeys_ref, lr_sem.at[2], lr_sem.at[3], sib)

    def flip(i):
        _, row = parts_of(keys_ref[i // 4, pl.ds((i % 4) * 2, 2)].reshape(128, 128))
        rowt_ref[:, at(i * 128, 128)] = row.T[0:8, :]

    lane_doc = lax.broadcasted_iota(jnp.int32, (64, BLK), 1).astype(F32)
    slot_l = (lax.broadcasted_iota(jnp.int32, (64, BLK), 0) % 8).astype(F32)

    def doc_pick(key):
        t, _ = parts_of(key)
        d = t - 16.0 * jnp.floor(t * (1.0 / 16.0)) + 16.0 * slot_l
        return lane_doc == jnp.where(key < BIG, d, -1.0)

    def target(i):
        out = []
        for q in range(4):
            b = i * 4 + q
            c, j = q % 2, i * 2 + q // 2
            key = keys_ref[c, j]
            t, _ = parts_of(key)
            found = mm(jnp.where(doc_pick(key), 1.0, 0.0).astype(BF16), dall[b])
            score = C * jnp.sum(found * lrow_ref[c, j].astype(F32), axis=1, keepdims=True)
            acc = [jnp.zeros((LB, 128), F32)] * 3
            for k in range(SLOTS):
                for v in range(3):
                    acc[v] = acc[v] + jnp.where(lane_t[v] == t[k * 8:k * 8 + 8], score[k * 8:k * 8 + 8], 0.0)
            out.append((b, c, j, found.astype(BF16), acc))
        for b, c, j, found, acc in out:
            grow_ref[c, j] = found
            for v in range(3):
                ts_ref[b, :, v * 128:(v + 1) * 128] = acc[v]

    def t1_copy(i):
        q, to = mate(i)
        return remote(ts_ref.at[q], tr_ref.at[dp], t1_send, t1_recv, to)


    def s1_copy(i):
        return remote(st_ref, sr_ref.at[lb], s1_send, s1_recv, (dp, (lb + i) % LB))

    def s2_copy(i):
        return remote(sv_ref.at[dp], sv_ref.at[dp], s2_send, s2_recv, mate(i)[1])

    def sst_copy():
        return remote(st_ref.at[0], sst_ref, sst_sem.at[0], sst_sem.at[1], sib)

    def merge(count, ref):
        tops = [ref[q, 0] for q in range(count)]
        top = functools.reduce(jnp.maximum, tops)
        total = 0.0
        for q in range(count):
            total = total + ref[q, 1] * jnp.exp(tops[q] - top)
        return top, total

    def stats_on():
        all_in(sr_ref.at[1:LB], s1_recv)
        sr_ref[lb] = st_ref[...]
        sv_ref[dp, 0], sv_ref[dp, 1] = merge(LB, sr_ref)
        each(1, DP, lambda i: s2_copy(i).start())

    def totals():
        all_in(sv_ref.at[1:DP], s2_recv)
        top, total = merge(DP, sv_ref)
        lt_ref[...] = top + jnp.log(total)

    def doc_part(g):
        part = mm(labt[...], e_ref[:, at(g * GRP, GRP)].astype(BF16))
        u_ref[at(g * GRP, GRP), :] = part.T

    def exp_group(p, g, top):
        total = 0.0
        for c in range(ROWS // CH):
            total = total + exp_rows(p, c, top, at(g * GRP, GRP))
        keep(g, top, total)

    def score_pair(i, top):
        top = score_step(i * 2, 0, top)

        @pl.when(i == 0)
        def _():
            exp_group(0, g_own, top)
            doc_part(g_own)
            ids_out()
            for k in (2, 3, 1):
                take(k)

        @pl.when(i == 1)
        def _():
            slot = doc_slot(place(1), co)
            relay_up(slot).start()
            relay_down(slot).start()

        @pl.when(i == 2)
        def _():
            take(5)
            take(6)
            each(2, 4, fetch)
            named_copy().start()
            keys_copy().start()
            each(0, 8, flip)

        @pl.when(i == 3)
        def _():
            wait_sib(7)
            each(0, 4, target)
            each(1, DP, lambda i: t1_copy(i).start())

        top = score_step(i * 2 + 1, 1, top)

        @pl.when(i == 1)
        def _():
            find()
            each(0, 1, fetch)
            take(4)
            each(1, 2, fetch)

        @pl.when(i == 2)
        def _():
            take(7)

        return top

    lg_ref[:, raw_cols(1)] = jnp.zeros((ROWS, GRP), F32)
    top = lax.fori_loop(0, 4, score_pair, jnp.zeros((1, GRP), F32))
    exp_group(1, place(7), top)

    each(1, LB, lambda i: s1_copy(i).start())
    sst_copy().start()

    def t2_copy(i):
        return remote(tu_ref, tv_ref.at[lb], t2_send, t2_recv, (dp, (lb + i) % LB))

    def t3_copy(i):
        return remote(ca_ref.at[dp], ca_ref.at[dp], t3_send, t3_recv, mate(i)[1])

    def targets_on():
        all_in(tr_ref.at[1:DP], t1_recv)
        tr_ref[dp] = ts_ref[dp]
        acc = tr_ref[0]
        for q in range(1, DP):
            acc = acc + tr_ref[q]
        tu_ref[...] = acc
        each(1, LB, lambda i: t2_copy(i).start())

    def coefficients_on():
        all_in(tv_ref.at[1:LB], t2_recv)
        tv_ref[lb] = tu_ref[...]
        acc = tv_ref[0]
        for q in range(1, LB):
            acc = acc + tv_ref[q]
        lane = lax.broadcasted_iota(jnp.int32, (LB, 128), 1)
        pos = jnp.where(lane < 16, acc[:, 0:128], 0.0)
        for s in (16, 32, 64):
            pos = pos + pltpu.roll(pos, s, 1)
        soft = jnp.zeros((LB, 128), F32)
        weight = jnp.zeros((LB, 128), F32)
        pieces = []
        for v in range(3):
            gap = acc[:, v * 128:(v + 1) * 128] - pos + 1.0
            use = (lane >= 16) if v == 0 else (lane >= 0) if v == 1 else (lane < 16)
            small = jnp.exp(-jnp.abs(gap))
            soft = soft + jnp.where(use, jnp.maximum(gap, 0.0) + jnp.log(1.0 + small), 0.0)
            sig = jnp.where(use, jnp.where(gap >= 0.0, 1.0, small) / (1.0 + small) * (1.0 / 16.0), 0.0)
            weight = weight + sig
            pieces.append(sig)
        for s in (16, 32, 64):
            soft = soft + pltpu.roll(soft, s, 1)
            weight = weight + pltpu.roll(weight, s, 1)
        tmp_ref[...] = soft * (1.0 / 16.0) - pos
        pieces[0] = jnp.where(lane < 16, -1.0 - weight, pieces[0])
        for v in range(3):
            ca_ref[dp, :, v * 128:(v + 1) * 128] = pieces[v]
        each(1, DP, lambda i: t3_copy(i).start())

    def core_copy(j):
        return remote(u_ref.at[at((j * 2 + 1 - co) * BLK, BLK), :], rc_ref.at[j], rc_send, rc_recv, sib)

    def doc_mm(k):
        doc_part(place(k))

        @pl.when(k == 3)
        def _():
            targets_on()
            stats_on()
            for j in range(4):
                core_copy(place(j)).start()

        @pl.when(k == 6)
        def _():
            coefficients_on()

        @pl.when(k > 3)
        def _():
            core_copy(place(k)).start()

    each(1, 8, doc_mm)
    totals()
    all_in(rc_ref, rc_recv)
    sst_copy().wait_recv()

    def column(row):
        return jnp.concatenate([jnp.broadcast_to(row, (BLK, BLK)).T] * (D // BLK), axis=1)

    def merge_cores(i):
        out = []
        for q in range(4):
            j = i * 4 + q
            b = j * 2 + co
            log_total = lt_ref[pl.ds(b, 1), :]
            col = column(jnp.exp(st_ref[0, pl.ds(b, 1), :] - log_total))
            scol = column(jnp.exp(sst_ref[pl.ds(b, 1), :] - log_total))
            out.append((b, u_ref[at(b * BLK, BLK), :] * col + rc_ref[j] * scol))
        for b, value in out:
            u_ref[at(b * BLK, BLK), :] = value

    each(0, 2, merge_cores)
    shifted = pltpu.roll(jnp.broadcast_to(lt_ref[pl.ds(dp, 1), :], (8, BLK)), (BLK - lb * SUB) % BLK, 1)
    loss_ref[...] = tmp_ref[pl.ds(lb, 1), :] + shifted[0:1, :]

    all_in(ca_ref.at[1:DP], t3_recv)

    def slot_coef(b, t):
        out = []
        for k in range(SLOTS):
            hit = [jnp.where(lane_t[v] == t[k * 8:k * 8 + 8], ca_ref[b, :, v * 128:(v + 1) * 128], 0.0) for v in range(3)]
            out.append(jnp.sum(hit[0] + hit[1] + hit[2], axis=1, keepdims=True))
        return jnp.concatenate(out, axis=0)

    def scaled_pick(key, coef):
        hi, lo = split(coef)
        pick = doc_pick(key)
        return [jnp.where(pick, hi, 0.0), jnp.where(pick, lo, 0.0)]

    def finish(i):
        out = []
        for q in range(4):
            j = i * 4 + q
            b = j * 2 + co
            key, skey = keys_ref[co, j], skeys_ref[j]
            coef, scoef = slot_coef(b, parts_of(key)[0]), slot_coef(b, parts_of(skey)[0])
            pick = jnp.concatenate(scaled_pick(key, coef) + scaled_pick(skey, scoef), axis=0).T.astype(BF16)
            named, snamed = lrow_ref[co, j], slr_ref[j]
            hard = mm(pick, jnp.concatenate([named, named, snamed, snamed], axis=0))
            out.append((j, coef, C * (u_ref[at(b * BLK, BLK), :] + hard)))
        for j, coef, value in out:
            coef_ref[co, j] = jnp.broadcast_to(coef, (64, 128))
            xx, hh = j // 2, j % 2
            for zz in range(NZ):
                for ll in range(NYL):
                    off = (zz * NYL + ll) * SUB
                    u = value[off:off + SUB]
                    yy = hh * 2 + ll
                    w_ref[0, xx, yy, zz] = u[:, 0:FG]
                    w_ref[1, yy, zz, xx] = u[:, FG:2 * FG]
                    w_ref[2, zz, xx, yy] = u[:, 2 * FG:3 * FG]

    named_copy().wait_recv()
    keys_copy().wait_recv()
    each(0, 2, finish)

    spot = (x, y, z)
    def ring_msg(f, m):
        h = spot[f]
        up, down = on_axis(f, (h + 1) % 4), on_axis(f, (h + 3) % 4)

        def part(block, which):
            return w_ref.at[f, block % 4, which * 2:which * 2 + 2]

        source = (part(h + 2, 0), part(h + 2, 1), part(h + 3, 1), part(h + 1, 0), q0_ref.at[f, 0], q0_ref.at[f, 1])[m]
        to = (down, up, down, up, down, up)[m]
        return remote(source, q0_ref.at[f, m], rs_send.at[0], rs_recv.at[0 if m < 2 else 1], to)

    def ring_start(msgs):
        for m in msgs:
            for f in range(3):
                ring_msg(f, m).start()

    def ring_relay():
        all_in(q0_ref.at[:, 0:2], rs_recv.at[0])
        for f in range(3):
            h = spot[f]
            for m in range(2):
                block = (h + 3) % 4 if m == 0 else (h + 1) % 4
                q0_ref[f, m] = q0_ref[f, m] + w_ref[f, block, m * 2:m * 2 + 2]
                ring_msg(f, 4 + m).start()

    def ring_done():
        all_in(q0_ref.at[:, 2:6], rs_recv.at[1])
        for f in range(3):
            h = spot[f]
            v1_ref[f, 0:2] = w_ref[f, h, 0:2] + q0_ref[f, 4] + q0_ref[f, 3]
            v1_ref[f, 2:4] = w_ref[f, h, 2:4] + q0_ref[f, 2] + q0_ref[f, 5]

    bufs = {1: (v1_ref, q1_ref), 2: (v2_ref, q2_ref)}

    def straight(step, f, i):
        axis = (f + step) % 3
        to = (spot[axis] + i) % 4
        src, box = bufs[step]
        return remote(src.at[f, to], box.at[f, i - 1], rs_send.at[step], rs_recv.at[step + 1], on_axis(axis, to))

    def straight_start(step):
        for i in (2, 1, 3):
            for f in range(3):
                straight(step, f, i).start()

    def straight_done(step):
        src, box = bufs[step]
        all_in(box, rs_recv.at[step + 1])
        return [src[f, spot[(f + step) % 3]] + box[f, 0] + box[f, 1] + box[f, 2] for f in range(3)]

    ring_start((0, 1))

    def coef_rows(i):
        hi, lo = split(coef_ref[i // 4, pl.ds((i % 4) * 2, 2)].reshape(128, 128).T[0:8, :])
        coeft_ref[0, :, at(i * 128, 128)] = hi
        coeft_ref[1, :, at(i * 128, 128)] = lo

    def other_coef(i):
        out = []
        for q in range(4):
            j = i * 4 + q
            out.append((j, slot_coef(j * 2 + 1 - co, parts_of(keys_ref[1 - co, j])[0])))
        for j, coef in out:
            coef_ref[1 - co, j] = jnp.broadcast_to(coef, (64, 128))

    each(0, 2, other_coef)
    each(0, 8, coef_rows)
    for b in range(DP):
        scale = jnp.exp(st_ref[0, b:b + 1, :] - lt_ref[b:b + 1, :])
        scale_ref[:, b * BLK:(b + 1) * BLK] = jnp.broadcast_to(scale, (8, BLK))

    def label_mm(r):
        probs = (e_ref[at(r * TILE, TILE), :] * scale_ref[0:1, :]).astype(BF16)
        sub_rows = (lax.broadcasted_iota(jnp.int32, (TILE, DEV * SLOTS), 0) + r * TILE).astype(F32)
        pick = sub_rows == rowt_ref[0:1, :]
        named = grow_ref[...].reshape(DEV * SLOTS, D)
        value = mm(probs, dall[...].reshape(DOCS, D))
        for p in range(2):
            value = value + mm(jnp.where(pick, coeft_ref[p, 0:1, :], 0.0).astype(BF16), named)
        lg_ref[at(r * TILE, TILE), :] = C * value

        @pl.when(r == 0)
        def _():
            ring_start((2, 3))

        @pl.when(r == 2)
        def _():
            ring_relay()

        @pl.when(r == 4)
        def _():
            ring_done()
            straight_start(1)

        @pl.when(r == 6)
        def _():
            for f, value in enumerate(straight_done(1)):
                v2_ref[f] = value
            straight_start(2)

    each(0, ROWS // TILE, label_mm)

    for f, value in enumerate(straight_done(2)):
        dg_ref[:, f * FG:(f + 1) * FG] = value

    all_out(dall.at[0:7], doc_send)
    all_out(dall.at[0:8], sib_send)
    all_out(rc_ref, rc_send)
    for copy in (sst_copy(), named_copy(), keys_copy()):
        copy.wait_send()
    all_out(idl_ref.at[1:LB], idl_send)
    all_out(idg_ref.at[1:DP], idg_send)
    all_out(sr_ref.at[1:LB], s1_send)
    all_out(sv_ref.at[1:DP], s2_send)
    all_out(tr_ref.at[1:DP], t1_send)
    all_out(tv_ref.at[1:LB], t2_send)
    all_out(ca_ref.at[1:DP], t3_send)
    all_out(q0_ref, rs_send.at[0])
    all_out(q1_ref, rs_send.at[1])
    all_out(q2_ref, rs_send.at[2])


def ship(lg_in, dg_in, loss_in, lg_out, dg_out, loss_out, sems):
    copies = [pltpu.make_async_copy(lg_in, lg_out, sems.at[0]), pltpu.make_async_copy(dg_in, dg_out, sems.at[1])]
    for copy in copies:
        copy.start()
    loss_out[...] = loss_in[0, 0:SUB]
    for copy in copies:
        copy.wait()


def shards(documents, labels, target_owner, target_row):
    vm = pl.BlockSpec(memory_space=pltpu.VMEM)
    hbm = pl.BlockSpec(memory_space=pl.ANY)
    dma = pltpu.SemaphoreType.DMA
    slots = DEV * SLOTS
    label_grad, doc_grad, loss = pl.pallas_call(
        kernel,
        out_shape=(
            pltpu.VMEM((ROWS, D), F32),
            pltpu.VMEM((SUB, D), F32),
            pltpu.VMEM((1, 128), F32),
        ),
        in_specs=[vm, hbm, vm, vm],
        out_specs=(vm, vm, vm),
        scratch_shapes=[
            pltpu.VMEM((ROWS, D), BF16),
            pltpu.VMEM((DP, BLK, D), BF16),
            pltpu.VMEM((D, ROWS), BF16),
            pltpu.VMEM((ROWS, DOCS), F32),
            pltpu.VMEM((DOCS, D), F32),
            pltpu.VMEM((8, BLK, D), F32),
            pltpu.VMEM((3, 4, 4, 4, SUB, FG), F32),
            pltpu.VMEM((3, 4, 4, SUB, FG), F32),
            pltpu.VMEM((3, 4, SUB, FG), F32),
            pltpu.VMEM((3, 6, 2, 4, SUB, FG), F32),
            pltpu.VMEM((3, 3, 4, SUB, FG), F32),
            pltpu.VMEM((3, 3, SUB, FG), F32),
            pltpu.VMEM((LB, TW), F32),
            pltpu.VMEM((LB, LB, TW), F32),
            pltpu.VMEM((DP, LB, TW), F32),
            pltpu.VMEM((2, 8, 64, 128), F32),
            pltpu.VMEM((8, 64, 128), F32),
            pltpu.VMEM((8, slots), F32),
            pltpu.VMEM((2, 8, 64, D), BF16),
            pltpu.VMEM((8, 64, D), BF16),
            pltpu.VMEM((2, 8, 64, D), BF16),
            pltpu.VMEM((2, DP, BLK), F32),
            pltpu.VMEM((LB, 2, DP, BLK), F32),
            pltpu.VMEM((DP, 2, DP, BLK), F32),
            pltpu.VMEM((DP, BLK), F32),
            pltpu.VMEM((DP, BLK), F32),
            pltpu.VMEM((DP, LB, TW), F32),
            pltpu.VMEM((DP, LB, TW), F32),
            pltpu.VMEM((LB, TW), F32),
            pltpu.VMEM((LB, LB, TW), F32),
            pltpu.VMEM((DP, LB, TW), F32),
            pltpu.VMEM((8, DOCS), F32),
            pltpu.VMEM((LB, 128), F32),
            pltpu.VMEM((2, 8, 64, 128), F32),
            pltpu.VMEM((2, 8, slots), F32),
            dma, dma, dma, dma((9,)), dma, dma((8,)),
            dma, dma, dma, dma,
            dma, dma, dma, dma, dma((2,)), dma((4,)),
            dma, dma, dma, dma, dma, dma,
            dma, dma, dma((3,)), dma((4,)),
        ],
        compiler_params=pltpu.CompilerParams(
            collective_id=0, has_side_effects=True, vmem_limit_bytes=56 * 1024 * 1024
        ),
        cost_estimate=pl.CostEstimate(
            flops=8 * ROWS * DOCS * D, bytes_accessed=10 * ROWS * D, transcendentals=ROWS * DOCS
        ),
        name="head",
    )(documents, labels, target_owner.transpose(0, 2, 1), target_row)
    label_grad, doc_grad, loss = pl.pallas_call(
        ship,
        out_shape=(
            jax.ShapeDtypeStruct((ROWS, D), F32),
            jax.ShapeDtypeStruct((SUB, D), F32),
            jax.ShapeDtypeStruct((SUB,), F32),
        ),
        in_specs=[vm, vm, vm],
        out_specs=(hbm, hbm, vm),
        scratch_shapes=[dma((2,))],
        compiler_params=pltpu.CompilerParams(vmem_limit_bytes=32 * 1024 * 1024),
        name="ship",
    )(label_grad, doc_grad, loss)
    return loss, doc_grad, label_grad


def solution(mesh):
    return jax.shard_map(
        shards,
        mesh=mesh,
        in_specs=(
            P("dp", None),
            P(("dp", "label"), None),
            P(("dp", "label"), None, None),
            P(("dp", "label"), None),
        ),
        out_specs=(P(("dp", "label")), P(("dp", "label"), None), P(("dp", "label"), None)),
        check_vma=False,
    )
```

time: 1480 us -> 75.8 us (0.05)
  waiting for transfers between devices: 1200 us -> 0 us
  local copies, waits for them, and re-layouts: 138 us -> 0 us
  Pallas kernels: 0 us -> 75 us
  matrix products: 39 us -> 0 us
  other arithmetic: 38 us -> 0 us
  blocking collectives: 18.8 us -> 0 us
    all_gather x3 -> x0, waiting for transfers between devices: 630 us -> none  [the longest x2 573 us: merged(): gathered = jax.tree.map(lambda a: lax.all_gather(a, axis), part)]
    reduce_scatter x1 -> x0, waiting for transfers between devices: 526 us -> none  [shards(): lax.psum_scatter(doc_part, ('dp', 'label'), scatter_dimension=0, tiled=True)]
    dynamic_slice x130 -> x0, local copies, waits for them, and re-layouts: 114 us -> none  [take(): lax.dynamic_index_in_dim(a, source, 0, False)]
    pallas_call x0 -> x2, Pallas kernels: none -> 75 us  [the longest x1 71.8 us: shards(): pl.pallas_call(kernel, out_shape=(pltpu.VMEM((ROWS, D), F32), pltpu.VMEM(...]
    all_to_all x2 -> x0, waiting for transfers between devices: 47.3 us -> none  [the longest x1 26.9 us: shards(): lax.all_to_all(send_grads, ('dp', 'label'), split_axis=0, concat_axis=0,...]
    dot_general x4 -> x0, matrix products: 39 us -> none  [the longest x1 13.2 us: shards(): lax.dot_general(probabilities, doc_piece, (((0,), (0,)), ((), ())), prefe...]
    all_to_all x1 -> x0, blocking collectives: 18.8 us -> none  [shards(): lax.all_to_all(send_rows, ('dp', 'label'), split_axis=0, concat_axis=0, t...]
  transfers between devices with their start and end apart: 6 -> 0, of which waited for: 6 -> 0; matrix products, arithmetic and copies ran while one was open for 5% -> 0% of each run, Pallas kernels for 0% -> 0%
where the time goes in v2:
time: 75.8 us; the launch traced here: 75.7 us
  Pallas kernels  75 us (99%)
    pallas_call x1, Pallas kernels, shards(): pl.pallas_call(kernel, out_shape=(pltpu.VMEM((ROWS, D), F32), pltpu.VMEM(...  71.8 us
    pallas_call x1, Pallas kernels, shards(): pl.pallas_call(ship, out_shape=(jax.ShapeDtypeStruct((ROWS, D), F32), jax...  3.23 us

profile of v2, /device:TPU:0, one launch (start us, length us, event | category | flops | bytes accessed | tf_op | source)
XLA Modules:
  0.0 75.7 jit_solution(52345594647814918)
XLA Ops:
  0.6 71.8 %head.1 = (f32[2048,768]{1,0:T(8,128)S(1)}, f32[16,768]{1,0:T(8,128)S(1)}, f32[1,128]{1,0:T(1,128)S(1)}) custom-call(bf16[128,768]{1,0:T(8,128)(2,1)} %docs_ref.1, bf16[2048,768]{1,0:T(8,128)(2,1)} %labels_hbm.1, s32[16,1,17]{2,1,0:T(1,128)} %bitcast.1, s32[16,17]{1,0:T(8,128)} %row_ref.1), custom_call_target="tpu_custom_call" | custom-call | flops 25769803776 | bytes 15728640 | tf_op jit(solution)/shard_map/head/pallas_call | solution.py:684
  72.4 3.2 %ship.1 = (f32[2048,768]{1,0:T(8,128)}, f32[16,768]{1,0:T(8,128)}, f32[16]{0:T(128)}) custom-call(f32[2048,768]{1,0:T(8,128)S(1)} %get-tuple-element.9.lg_in, f32[16,768]{1,0:T(8,128)S(1)} %get-tuple-element.10.dg_in, f32[1,128]{1,0:T(1,128)S(1)} %get-tuple-element.11.loss_in), custom_call_target="tpu_custom_call" | custom-call | tf_op jit(solution)/shard_map/ship/pallas_call | solution.py:743

commit v3 on v2

--- a/solution.py
+++ b/solution.py
@@ -42,13 +42,13 @@
 
 
 def kernel(
-    docs_ref, labels_hbm, owner_ref, row_ref,
+    docs_hbm, labels_hbm, owner_hbm, row_hbm,
     lg_ref, dg_ref, loss_ref,
     lab, dall, labt, e_ref, u_ref, rc_ref, w_ref, v1_ref, v2_ref, q0_ref, q1_ref, q2_ref,
-    ids_ref, idl_ref, idg_ref, keys_ref, skeys_ref, rowt_ref, lrow_ref, slr_ref, grow_ref,
+    owner_ref, row_ref, ids_ref, idl_ref, idg_ref, keys_ref, skeys_ref, rowt_ref, lrow_ref, slr_ref, grow_ref,
     st_ref, sr_ref, sv_ref, sst_ref, lt_ref,
     ts_ref, tr_ref, tu_ref, tv_ref, ca_ref, scale_ref, tmp_ref, coef_ref, coeft_ref,
-    lab_sem, own_sem, doc_send, doc_recv, sib_send, sib_recv,
+    lab_sem, own_sem, in_sem, doc_send, doc_recv, sib_send, sib_recv,
     idl_send, idl_recv, idg_send, idg_recv,
     s1_send, s1_recv, s2_send, s2_recv, sst_sem, lr_sem,
     t1_send, t1_recv, t2_send, t2_recv, t3_send, t3_recv,
@@ -116,8 +116,76 @@
     def doc_slot(group, core):
         return dall.at[group * 2 + core]
 
-    own_copy = pltpu.make_async_copy(docs_ref, doc_slot(g_own, co), own_sem)
+    own_copy = pltpu.make_async_copy(docs_hbm, doc_slot(g_own, co), own_sem)
     own_copy.start()
+    id_copies = [
+        pltpu.make_async_copy(owner_hbm, owner_ref, in_sem.at[0]),
+        pltpu.make_async_copy(row_hbm, row_ref, in_sem.at[1]),
+    ]
+    for copy in id_copies:
+        copy.start()
+    pl.semaphore_wait(barrier, DP - 1 + LB - 1 + 1)
+
+    def sib_copy(k, src, group):
+        return remote(src, doc_slot(group, co), sib_send, sib_recv.at[k], sib)
+
+    own_copy.wait()
+    sib_copy(0, doc_slot(g_own, co), g_own).start()
+    def some(ref, start, size):
+        return ref.at[start:start + size, :]
+
+    def half_copy(h, rsem, to):
+        block = some(doc_slot(g_own, co), h * 64, 64)
+        return remote(block, block, doc_send, doc_recv.at[rsem], to)
+
+    remote(doc_slot(g_own, co), doc_slot(g_own, co), doc_send, doc_recv.at[3], ypart).start()
+    half_copy(0, 1, xdown).start()
+    half_copy(1, 2, xup).start()
+
+    def place(k):
+        dx = jnp.where((k == 1) | (k == 5), 1, jnp.where((k == 2) | (k == 6), 3, jnp.where((k == 4) | (k == 7), 2, 0)))
+        dy = jnp.where((k == 3) | (k >= 5), 1, 0)
+        return ((x + dx) % NX) * 2 + (yh + dy) % 2
+
+    def relay_up(slot):
+        return remote(slot, slot, doc_send, doc_recv.at[6], xup)
+
+    def relay_down(slot):
+        return remote(slot, slot, doc_send, doc_recv.at[5], xdown)
+
+    def relay_far(slot, h):
+        block = some(slot, h * 64, 64)
+        return remote(block, block, doc_send, doc_recv.at[(4, 9)[h]], xup if h else xdown)
+
+    def relay_y(slot):
+        return remote(slot, slot, doc_send, doc_recv.at[7], ypart)
+
+    def part_in(k, start, size, rsem):
+        block = some(doc_slot(place(k), co), start, size)
+        remote(block, block, doc_send, doc_recv.at[rsem], ypart).wait_recv()
+
+    def far():
+        part_in(1, 0, 64, 1)
+        part_in(2, 64, 64, 2)
+        for h in range(2):
+            relay_far(doc_slot(place(1 + h), co), h).start()
+
+    def take(k):
+        slot = doc_slot(place(k), co)
+        if k == 1:
+            part_in(1, 64, 64, 12)
+        elif k == 2:
+            part_in(2, 0, 64, 8)
+        elif k == 4:
+            part_in(4, 0, 64, 4)
+            part_in(4, 64, 64, 9)
+            relay_y(slot).start()
+        else:
+            remote(slot, slot, doc_send, doc_recv.at[k], ypart).wait_recv()
+        sib_copy(k, slot, place(k)).start()
+
+    for copy in id_copies:
+        copy.wait()
     named = (owner_ref[:, 0, :] * ROWS + row_ref[...]).astype(F32)
     high = jnp.floor(named * (1.0 / 4096.0))
     rest = named - 4096.0 * high
@@ -130,64 +198,10 @@
     own = jnp.sum(jnp.where(lane % SUB == lax.broadcasted_iota(jnp.int32, (SUB, TW), 0), spread, 0.0), axis=0, keepdims=True)
     own = jnp.where(lane[0:1] < SUB * COLS, own, -1.0)
     ids_ref[...] = jnp.where(lax.broadcasted_iota(jnp.int32, (LB, TW), 0) == lb, own, 0.0)
-    pl.semaphore_wait(barrier, DP - 1 + LB - 1 + 1)
-
     def idl_copy(i):
         return remote(ids_ref, idl_ref.at[lb], idl_send, idl_recv, (dp, (lb + i) % LB))
 
     each(1, LB, lambda i: idl_copy(i).start())
-
-    def sib_copy(k, src, group):
-        return remote(src, doc_slot(group, co), sib_send, sib_recv.at[k], sib)
-
-    sib_copy(0, docs_ref, g_own).start()
-    first_sends = [
-        remote(docs_ref, doc_slot(g_own, co), doc_send, doc_recv.at[1], ypart),
-        remote(docs_ref, doc_slot(g_own, co), doc_send, doc_recv.at[3], xup),
-        remote(docs_ref, doc_slot(g_own, co), doc_send, doc_recv.at[2], xdown),
-    ]
-    for copy in first_sends:
-        copy.start()
-
-    def place(k):
-        dx = jnp.where((k == 2) | (k == 5), 1, jnp.where((k == 3) | (k == 6), 3, jnp.where((k == 4) | (k == 7), 2, 0)))
-        dy = jnp.where((k == 1) | (k >= 5), 1, 0)
-        return ((x + dx) % NX) * 2 + (yh + dy) % 2
-
-    def half(ref, h):
-        return ref.at[h * (BLK // 2):(h + 1) * (BLK // 2), :]
-
-    def relay_up(slot):
-        return remote(slot, slot, doc_send, doc_recv.at[6], xup)
-
-    def relay_down(slot):
-        return remote(slot, slot, doc_send, doc_recv.at[5], xdown)
-
-    def relay_far_a(slot):
-        return remote(half(slot, 0), half(slot, 0), doc_send, doc_recv.at[4], xdown)
-
-    def relay_far_b(slot):
-        return remote(half(slot, 1), half(slot, 1), doc_send, doc_recv.at[8], xup)
-
-    def relay_y(slot):
-        return remote(slot, slot, doc_send, doc_recv.at[7], ypart)
-
-    def take(k):
-        slot = doc_slot(place(k), co)
-
-        if k != 4:
-            remote(slot, slot, doc_send, doc_recv.at[k], ypart).wait_recv()
-        else:
-            for h in range(2):
-                remote(half(slot, h), half(slot, h), doc_send, doc_recv.at[4 + 4 * h], ypart).wait_recv()
-
-        if k == 2:
-            relay_far_a(slot).start()
-        if k == 3:
-            relay_far_b(slot).start()
-        if k == 4:
-            relay_y(slot).start()
-        sib_copy(k, slot, place(k)).start()
 
     ts_ref[...] = jnp.zeros_like(ts_ref)
     st_ref[...] = jnp.zeros_like(st_ref)
@@ -197,13 +211,14 @@
         labt[:, at(i * 256, 256)] = lab[at(i * 256, 256), :].T
 
     each(0, ROWS // 256, turn)
-
-    own_copy.wait()
+    half_copy(1, 12, xdown).start()
+    half_copy(0, 8, xup).start()
+
 
     def raw_cols(p):
         return slice(p * GRP, (p + 1) * GRP)
 
-    CH = 512
+    CH = 256
 
     def exp_rows(p, c, top, cols):
         s = lg_ref[c * CH:(c + 1) * CH, raw_cols(p)]
@@ -223,7 +238,7 @@
     def score_step(k, p, old_top):
         g = place(k)
 
-        @pl.when(k < 7)
+        @pl.when(k < 5)
         def _():
             wait_sib(k)
 
@@ -272,12 +287,15 @@
         row = jnp.where(key < BIG, key - t * float(ROWS), -1.0)
         return t, row
 
-    def fetch(i):
+    def fetch(c):
         lane_rows = lax.broadcasted_iota(jnp.int32, (256, ROWS), 1).astype(F32)
-        c, j = i // 2, pl.ds((i % 2) * 4, 4)
-        _, row = parts_of(keys_ref[c, j].reshape(256, 128)[:, 0:1])
-        pick = jnp.where(lane_rows == row, 1.0, 0.0).astype(BF16)
-        lrow_ref[c, j] = mm(pick, lab[...]).astype(BF16).reshape(4, 64, D)
+        out = []
+        for h in range(2):
+            _, row = parts_of(keys_ref[c, h * 4:h * 4 + 4].reshape(256, 128)[:, 0:1])
+            pick = jnp.where(lane_rows == row, 1.0, 0.0).astype(BF16)
+            out.append(mm(pick, lab[...]).astype(BF16).reshape(4, 64, D))
+        for h in range(2):
+            lrow_ref[c, h * 4:h * 4 + 4] = out[h]
 
     def named_copy():
         return remote(lrow_ref.at[1 - co], slr_ref, lr_sem.at[0], lr_sem.at[1], sib)
@@ -306,15 +324,14 @@
             t, _ = parts_of(key)
             found = mm(jnp.where(doc_pick(key), 1.0, 0.0).astype(BF16), dall[b])
             score = C * jnp.sum(found * lrow_ref[c, j].astype(F32), axis=1, keepdims=True)
-            acc = [jnp.zeros((LB, 128), F32)] * 3
+            slots = jnp.full((LB, 128), -1.0, F32)
             for k in range(SLOTS):
-                for v in range(3):
-                    acc[v] = acc[v] + jnp.where(lane_t[v] == t[k * 8:k * 8 + 8], score[k * 8:k * 8 + 8], 0.0)
-            out.append((b, c, j, found.astype(BF16), acc))
-        for b, c, j, found, acc in out:
+                slots = jnp.where(lane_8 == float(k), score[k * 8:k * 8 + 8], slots)
+                slots = jnp.where(lane_8 == float(SLOTS + k), t[k * 8:k * 8 + 8], slots)
+            out.append((b, c, j, found.astype(BF16), slots))
+        for b, c, j, found, slots in out:
             grow_ref[c, j] = found
-            for v in range(3):
-                ts_ref[b, :, v * 128:(v + 1) * 128] = acc[v]
+            ts_ref[b] = slots
 
     def t1_copy(i):
         q, to = mate(i)
@@ -322,7 +339,7 @@
 
 
     def s1_copy(i):
-        return remote(st_ref, sr_ref.at[lb], s1_send, s1_recv, (dp, (lb + i) % LB))
+        return remote(st_ref.at[1], sr_ref.at[lb], s1_send, s1_recv, (dp, (lb + i) % LB))
 
     def s2_copy(i):
         return remote(sv_ref.at[dp], sv_ref.at[dp], s2_send, s2_recv, mate(i)[1])
@@ -331,23 +348,25 @@
         return remote(st_ref.at[0], sst_ref, sst_sem.at[0], sst_sem.at[1], sib)
 
     def merge(count, ref):
-        tops = [ref[q, 0] for q in range(count)]
+        tops = [ref[q] for q in range(count)]
         top = functools.reduce(jnp.maximum, tops)
         total = 0.0
         for q in range(count):
-            total = total + ref[q, 1] * jnp.exp(tops[q] - top)
-        return top, total
+            total = total + jnp.exp(tops[q] - top)
+        return top + jnp.log(total)
 
     def stats_on():
         all_in(sr_ref.at[1:LB], s1_recv)
-        sr_ref[lb] = st_ref[...]
-        sv_ref[dp, 0], sv_ref[dp, 1] = merge(LB, sr_ref)
+        sr_ref[lb] = st_ref[1]
+        sv_ref[dp] = merge(LB, sr_ref)
         each(1, DP, lambda i: s2_copy(i).start())
 
     def totals():
         all_in(sv_ref.at[1:DP], s2_recv)
-        top, total = merge(DP, sv_ref)
-        lt_ref[...] = top + jnp.log(total)
+        lt_ref[...] = merge(DP, sv_ref)
+
+    def core_copy(j):
+        return remote(u_ref.at[at((j * 2 + 1 - co) * BLK, BLK), :], rc_ref.at[j], rc_send, rc_recv, sib)
 
     def doc_part(g):
         part = mm(labt[...], e_ref[:, at(g * GRP, GRP)].astype(BF16))
@@ -360,34 +379,35 @@
         keep(g, top, total)
 
     def score_pair(i, top):
+        @pl.when(i == 1)
+        def _():
+            slot = doc_slot(place(3), co)
+            relay_up(slot).start()
+            relay_down(slot).start()
+
         top = score_step(i * 2, 0, top)
 
         @pl.when(i == 0)
         def _():
             exp_group(0, g_own, top)
             doc_part(g_own)
+            core_copy(g_own).start()
+            far()
             ids_out()
-            for k in (2, 3, 1):
+            for k in (1, 2, 3):
                 take(k)
 
-        @pl.when(i == 1)
-        def _():
-            slot = doc_slot(place(1), co)
-            relay_up(slot).start()
-            relay_down(slot).start()
-
         @pl.when(i == 2)
         def _():
+            find()
+            fetch(0)
             take(5)
             take(6)
-            each(2, 4, fetch)
-            named_copy().start()
-            keys_copy().start()
+            fetch(1)
+            take(7)
             each(0, 8, flip)
-
-        @pl.when(i == 3)
-        def _():
-            wait_sib(7)
+            for k in (5, 6, 7):
+                wait_sib(k)
             each(0, 4, target)
             each(1, DP, lambda i: t1_copy(i).start())
 
@@ -395,14 +415,7 @@
 
         @pl.when(i == 1)
         def _():
-            find()
-            each(0, 1, fetch)
             take(4)
-            each(1, 2, fetch)
-
-        @pl.when(i == 2)
-        def _():
-            take(7)
 
         return top
 
@@ -410,6 +423,7 @@
     top = lax.fori_loop(0, 4, score_pair, jnp.zeros((1, GRP), F32))
     exp_group(1, place(7), top)
 
+    st_ref[1] = st_ref[0] + jnp.log(st_ref[1])
     each(1, LB, lambda i: s1_copy(i).start())
     sst_copy().start()
 
@@ -422,10 +436,15 @@
     def targets_on():
         all_in(tr_ref.at[1:DP], t1_recv)
         tr_ref[dp] = ts_ref[dp]
-        acc = tr_ref[0]
-        for q in range(1, DP):
-            acc = acc + tr_ref[q]
-        tu_ref[...] = acc
+        acc = [jnp.zeros((LB, 128), F32)] * 3
+        for q in range(DP):
+            slots = tr_ref[q]
+            for k in range(SLOTS):
+                score, t = slots[:, k:k + 1], slots[:, SLOTS + k:SLOTS + k + 1]
+                for v in range(3):
+                    acc[v] = acc[v] + jnp.where(lane_t[v] == t, score, 0.0)
+        for v in range(3):
+            tu_ref[:, v * 128:(v + 1) * 128] = acc[v]
         each(1, LB, lambda i: t2_copy(i).start())
 
     def coefficients_on():
@@ -458,26 +477,19 @@
             ca_ref[dp, :, v * 128:(v + 1) * 128] = pieces[v]
         each(1, DP, lambda i: t3_copy(i).start())
 
-    def core_copy(j):
-        return remote(u_ref.at[at((j * 2 + 1 - co) * BLK, BLK), :], rc_ref.at[j], rc_send, rc_recv, sib)
+    targets_on()
+    named_copy().start()
+    keys_copy().start()
 
     def doc_mm(k):
         doc_part(place(k))
 
-        @pl.when(k == 3)
-        def _():
-            targets_on()
+        core_copy(place(k)).start()
+
+        @pl.when(k == 4)
+        def _():
             stats_on()
-            for j in range(4):
-                core_copy(place(j)).start()
-
-        @pl.when(k == 6)
-        def _():
             coefficients_on()
-
-        @pl.when(k > 3)
-        def _():
-            core_copy(place(k)).start()
 
     each(1, 8, doc_mm)
     totals()
@@ -545,33 +557,39 @@
     each(0, 2, finish)
 
     spot = (x, y, z)
-    def ring_msg(f, m):
+    def ring_msg(f, m, p=None):
         h = spot[f]
         up, down = on_axis(f, (h + 1) % 4), on_axis(f, (h + 3) % 4)
 
         def part(block, which):
-            return w_ref.at[f, block % 4, which * 2:which * 2 + 2]
-
-        source = (part(h + 2, 0), part(h + 2, 1), part(h + 3, 1), part(h + 1, 0), q0_ref.at[f, 0], q0_ref.at[f, 1])[m]
+            if p is None:
+                return w_ref.at[f, block % 4, which * 2:which * 2 + 2]
+            return w_ref.at[f, block % 4, which * 2 + p]
+
+        box = q0_ref.at[f, m] if p is None else q0_ref.at[f, m, p]
+        if m >= 4:
+            source = q0_ref.at[f, m - 4, p]
+        else:
+            source = (part(h + 2, 0), part(h + 2, 1), part(h + 3, 1), part(h + 1, 0))[m]
         to = (down, up, down, up, down, up)[m]
-        return remote(source, q0_ref.at[f, m], rs_send.at[0], rs_recv.at[0 if m < 2 else 1], to)
-
-    def ring_start(msgs):
+        return remote(source, box, rs_send.at[0], rs_recv.at[2 if m >= 2 else p], to)
+
+    def ring_start(msgs, p=None):
         for m in msgs:
             for f in range(3):
-                ring_msg(f, m).start()
-
-    def ring_relay():
-        all_in(q0_ref.at[:, 0:2], rs_recv.at[0])
+                ring_msg(f, m, p).start()
+
+    def ring_relay(p):
+        all_in(q0_ref.at[:, 0:2, p], rs_recv.at[p])
         for f in range(3):
             h = spot[f]
             for m in range(2):
                 block = (h + 3) % 4 if m == 0 else (h + 1) % 4
-                q0_ref[f, m] = q0_ref[f, m] + w_ref[f, block, m * 2:m * 2 + 2]
-                ring_msg(f, 4 + m).start()
+                q0_ref[f, m, p] = q0_ref[f, m, p] + w_ref[f, block, m * 2 + p]
+                ring_msg(f, 4 + m, p).start()
 
     def ring_done():
-        all_in(q0_ref.at[:, 2:6], rs_recv.at[1])
+        all_in(q0_ref.at[:, 2:6], rs_recv.at[2])
         for f in range(3):
             h = spot[f]
             v1_ref[f, 0:2] = w_ref[f, h, 0:2] + q0_ref[f, 4] + q0_ref[f, 3]
@@ -583,7 +601,7 @@
         axis = (f + step) % 3
         to = (spot[axis] + i) % 4
         src, box = bufs[step]
-        return remote(src.at[f, to], box.at[f, i - 1], rs_send.at[step], rs_recv.at[step + 1], on_axis(axis, to))
+        return remote(src.at[f, to], box.at[f, i - 1], rs_send.at[step], rs_recv.at[step + 2], on_axis(axis, to))
 
     def straight_start(step):
         for i in (2, 1, 3):
@@ -592,10 +610,10 @@
 
     def straight_done(step):
         src, box = bufs[step]
-        all_in(box, rs_recv.at[step + 1])
+        all_in(box, rs_recv.at[step + 2])
         return [src[f, spot[(f + step) % 3]] + box[f, 0] + box[f, 1] + box[f, 2] for f in range(3)]
 
-    ring_start((0, 1))
+    ring_start((0, 1), 0)
 
     def coef_rows(i):
         hi, lo = split(coef_ref[i // 4, pl.ds((i % 4) * 2, 2)].reshape(128, 128).T[0:8, :])
@@ -610,6 +628,7 @@
         for j, coef in out:
             coef_ref[1 - co, j] = jnp.broadcast_to(coef, (64, 128))
 
+    ring_start((0, 1), 1)
     each(0, 2, other_coef)
     each(0, 8, coef_rows)
     for b in range(DP):
@@ -617,22 +636,27 @@
         scale_ref[:, b * BLK:(b + 1) * BLK] = jnp.broadcast_to(scale, (8, BLK))
 
     def label_mm(r):
-        probs = (e_ref[at(r * TILE, TILE), :] * scale_ref[0:1, :]).astype(BF16)
+        rows = at(r * TILE, TILE)
+        probs = (e_ref[rows, :] * scale_ref[0:1, :]).astype(BF16)
         sub_rows = (lax.broadcasted_iota(jnp.int32, (TILE, DEV * SLOTS), 0) + r * TILE).astype(F32)
         pick = sub_rows == rowt_ref[0:1, :]
         named = grow_ref[...].reshape(DEV * SLOTS, D)
         value = mm(probs, dall[...].reshape(DOCS, D))
         for p in range(2):
             value = value + mm(jnp.where(pick, coeft_ref[p, 0:1, :], 0.0).astype(BF16), named)
-        lg_ref[at(r * TILE, TILE), :] = C * value
+        lg_ref[rows, :] = C * value
 
         @pl.when(r == 0)
         def _():
             ring_start((2, 3))
 
+        @pl.when(r == 1)
+        def _():
+            ring_relay(0)
+
         @pl.when(r == 2)
         def _():
-            ring_relay()
+            ring_relay(1)
 
         @pl.when(r == 4)
         def _():
@@ -688,7 +712,7 @@
             pltpu.VMEM((SUB, D), F32),
             pltpu.VMEM((1, 128), F32),
         ),
-        in_specs=[vm, hbm, vm, vm],
+        in_specs=[hbm, hbm, hbm, hbm],
         out_specs=(vm, vm, vm),
         scratch_shapes=[
             pltpu.VMEM((ROWS, D), BF16),
@@ -703,6 +727,8 @@
             pltpu.VMEM((3, 6, 2, 4, SUB, FG), F32),
             pltpu.VMEM((3, 3, 4, SUB, FG), F32),
             pltpu.VMEM((3, 3, SUB, FG), F32),
+            pltpu.VMEM((SUB, 1, COLS), jnp.int32),
+            pltpu.VMEM((SUB, COLS), jnp.int32),
             pltpu.VMEM((LB, TW), F32),
             pltpu.VMEM((LB, LB, TW), F32),
             pltpu.VMEM((DP, LB, TW), F32),
@@ -713,12 +739,12 @@
             pltpu.VMEM((8, 64, D), BF16),
             pltpu.VMEM((2, 8, 64, D), BF16),
             pltpu.VMEM((2, DP, BLK), F32),
-            pltpu.VMEM((LB, 2, DP, BLK), F32),
-            pltpu.VMEM((DP, 2, DP, BLK), F32),
+            pltpu.VMEM((LB, DP, BLK), F32),
+            pltpu.VMEM((DP, DP, BLK), F32),
             pltpu.VMEM((DP, BLK), F32),
             pltpu.VMEM((DP, BLK), F32),
-            pltpu.VMEM((DP, LB, TW), F32),
-            pltpu.VMEM((DP, LB, TW), F32),
+            pltpu.VMEM((DP, LB, 128), F32),
+            pltpu.VMEM((DP, LB, 128), F32),
             pltpu.VMEM((LB, TW), F32),
             pltpu.VMEM((LB, LB, TW), F32),
             pltpu.VMEM((DP, LB, TW), F32),
@@ -726,11 +752,11 @@
             pltpu.VMEM((LB, 128), F32),
             pltpu.VMEM((2, 8, 64, 128), F32),
             pltpu.VMEM((2, 8, slots), F32),
-            dma, dma, dma, dma((9,)), dma, dma((8,)),
+            dma, dma, dma((2,)), dma, dma((13,)), dma, dma((8,)),
             dma, dma, dma, dma,
             dma, dma, dma, dma, dma((2,)), dma((4,)),
             dma, dma, dma, dma, dma, dma,
-            dma, dma, dma((3,)), dma((4,)),
+            dma, dma, dma((3,)), dma((5,)),
         ],
         compiler_params=pltpu.CompilerParams(
             collective_id=0, has_side_effects=True, vmem_limit_bytes=56 * 1024 * 1024

time: 75.8 us -> 72.6 us (0.958)
  Pallas kernels: 75 us -> 71.8 us
    pallas_call x1, Pallas kernels: 71.8 us -> 68.5 us  [shards(): pl.pallas_call(kernel, out_shape=(pltpu.VMEM((ROWS, D), F32), pltpu.VMEM(...]
where the time goes in v3:
time: 72.6 us; the launch traced here: 72.4 us
  Pallas kernels  71.8 us (99%)
    pallas_call x1, Pallas kernels, shards(): pl.pallas_call(kernel, out_shape=(pltpu.VMEM((ROWS, D), F32), pltpu.VMEM(...  68.5 us
    pallas_call x1, Pallas kernels, shards(): pl.pallas_call(ship, out_shape=(jax.ShapeDtypeStruct((ROWS, D), F32), jax...  3.23 us

profile of v3, /device:TPU:0, one launch (start us, length us, event | category | flops | bytes accessed | tf_op | source)
XLA Modules:
  0.0 72.4 jit_solution(6531339182285189711)
XLA Ops:
  0.6 68.5 %head.1 = (f32[2048,768]{1,0:T(8,128)S(1)}, f32[16,768]{1,0:T(8,128)S(1)}, f32[1,128]{1,0:T(1,128)S(1)}) custom-call(bf16[128,768]{1,0:T(8,128)(2,1)} %docs_hbm.1, bf16[2048,768]{1,0:T(8,128)(2,1)} %labels_hbm.1, s32[16,1,17]{2,1,0:T(1,128)} %bitcast.1, s32[16,17]{1,0:T(8,128)} %row_hbm.1), custom_call_target="tpu_custom_call" | custom-call | flops 25769803776 | bytes 15728640 | tf_op jit(solution)/shard_map/head/pallas_call | solution.py:708
  69.2 3.2 %ship.1 = (f32[2048,768]{1,0:T(8,128)}, f32[16,768]{1,0:T(8,128)}, f32[16]{0:T(128)}) custom-call(f32[2048,768]{1,0:T(8,128)S(1)} %get-tuple-element.9.lg_in, f32[16,768]{1,0:T(8,128)S(1)} %get-tuple-element.10.dg_in, f32[1,128]{1,0:T(1,128)S(1)} %get-tuple-element.11.loss_in), custom_call_target="tpu_custom_call" | custom-call | tf_op jit(solution)/shard_map/ship/pallas_call | solution.py:769

commit v4 on v3

--- a/solution.py
+++ b/solution.py
@@ -192,7 +192,7 @@
     mid = jnp.floor(rest * (1.0 / 64.0))
     digits = jnp.concatenate([high, mid, rest - 64.0 * mid], axis=0).astype(BF16)
     lane = lax.broadcasted_iota(jnp.int32, (COLS, TW), 1)
-    spread = mm(digits, jnp.where(lane // SUB == lax.broadcasted_iota(jnp.int32, (COLS, TW), 0), 1.0, 0.0).astype(BF16))
+    spread = mm(digits, jnp.where((lane // SUB + 1) % COLS == lax.broadcasted_iota(jnp.int32, (COLS, TW), 0), 1.0, 0.0).astype(BF16))
     spread = 4096.0 * spread[0:SUB] + 64.0 * spread[SUB:2 * SUB] + spread[2 * SUB:3 * SUB]
     lane = lax.broadcasted_iota(jnp.int32, (SUB, TW), 1)
     own = jnp.sum(jnp.where(lane % SUB == lax.broadcasted_iota(jnp.int32, (SUB, TW), 0), spread, 0.0), axis=0, keepdims=True)
@@ -318,8 +318,8 @@
     def target(i):
         out = []
         for q in range(4):
-            b = i * 4 + q
-            c, j = q % 2, i * 2 + q // 2
+            c, j = q % 2, place(i * 2 + q // 2)
+            b = j * 2 + c
             key = keys_ref[c, j]
             t, _ = parts_of(key)
             found = mm(jnp.where(doc_pick(key), 1.0, 0.0).astype(BF16), dall[b])
@@ -405,11 +405,19 @@
             take(6)
             fetch(1)
             take(7)
+            wait_sib(5)
+
+            def targets(i):
+                @pl.when(i == 3)
+                def _():
+                    wait_sib(6)
+                    wait_sib(7)
+
+                target(i)
+
+            each(0, 4, targets)
+            each(1, DP, lambda i: t1_copy(i).start())
             each(0, 8, flip)
-            for k in (5, 6, 7):
-                wait_sib(k)
-            each(0, 4, target)
-            each(1, DP, lambda i: t1_copy(i).start())
 
         top = score_step(i * 2 + 1, 1, top)
 
@@ -431,7 +439,7 @@
         return remote(tu_ref, tv_ref.at[lb], t2_send, t2_recv, (dp, (lb + i) % LB))
 
     def t3_copy(i):
-        return remote(ca_ref.at[dp], ca_ref.at[dp], t3_send, t3_recv, mate(i)[1])
+        return remote(ca_ref.at[dp, :, 0:256], ca_ref.at[dp, :, 0:256], t3_send, t3_recv, mate(i)[1])
 
     def targets_on():
         all_in(tr_ref.at[1:DP], t1_recv)
@@ -447,6 +455,15 @@
             tu_ref[:, v * 128:(v + 1) * 128] = acc[v]
         each(1, LB, lambda i: t2_copy(i).start())
 
+    def spread_16(value):
+        for shift in (16, 32, 64):
+            value = value + pltpu.roll(value, shift, 1)
+        return value
+
+    def positives():
+        for q in range(DP):
+            ca_ref[q, :, 256:384] = -1.0 - spread_16(ca_ref[q, :, 0:128] + ca_ref[q, :, 128:256])
+
     def coefficients_on():
         all_in(tv_ref.at[1:LB], t2_recv)
         tv_ref[lb] = tu_ref[...]
@@ -454,27 +471,14 @@
         for q in range(1, LB):
             acc = acc + tv_ref[q]
         lane = lax.broadcasted_iota(jnp.int32, (LB, 128), 1)
-        pos = jnp.where(lane < 16, acc[:, 0:128], 0.0)
-        for s in (16, 32, 64):
-            pos = pos + pltpu.roll(pos, s, 1)
+        pos = spread_16(jnp.where(lane < SUB, acc[:, 256:384], 0.0))
         soft = jnp.zeros((LB, 128), F32)
-        weight = jnp.zeros((LB, 128), F32)
-        pieces = []
-        for v in range(3):
+        for v in range(2):
             gap = acc[:, v * 128:(v + 1) * 128] - pos + 1.0
-            use = (lane >= 16) if v == 0 else (lane >= 0) if v == 1 else (lane < 16)
             small = jnp.exp(-jnp.abs(gap))
-            soft = soft + jnp.where(use, jnp.maximum(gap, 0.0) + jnp.log(1.0 + small), 0.0)
-            sig = jnp.where(use, jnp.where(gap >= 0.0, 1.0, small) / (1.0 + small) * (1.0 / 16.0), 0.0)
-            weight = weight + sig
-            pieces.append(sig)
-        for s in (16, 32, 64):
-            soft = soft + pltpu.roll(soft, s, 1)
-            weight = weight + pltpu.roll(weight, s, 1)
-        tmp_ref[...] = soft * (1.0 / 16.0) - pos
-        pieces[0] = jnp.where(lane < 16, -1.0 - weight, pieces[0])
-        for v in range(3):
-            ca_ref[dp, :, v * 128:(v + 1) * 128] = pieces[v]
+            soft = soft + jnp.maximum(gap, 0.0) + jnp.log(1.0 + small)
+            ca_ref[dp, :, v * 128:(v + 1) * 128] = jnp.where(gap >= 0.0, 1.0, small) / (1.0 + small) * (1.0 / 16.0)
+        tmp_ref[...] = spread_16(soft) * (1.0 / 16.0) - pos
         each(1, DP, lambda i: t3_copy(i).start())
 
     targets_on()
@@ -515,7 +519,8 @@
     shifted = pltpu.roll(jnp.broadcast_to(lt_ref[pl.ds(dp, 1), :], (8, BLK)), (BLK - lb * SUB) % BLK, 1)
     loss_ref[...] = tmp_ref[pl.ds(lb, 1), :] + shifted[0:1, :]
 
-    all_in(ca_ref.at[1:DP], t3_recv)
+    all_in(ca_ref.at[1:DP, :, 0:256], t3_recv)
+    positives()
 
     def slot_coef(b, t):
         out = []
@@ -685,7 +690,7 @@
     all_out(sv_ref.at[1:DP], s2_send)
     all_out(tr_ref.at[1:DP], t1_send)
     all_out(tv_ref.at[1:LB], t2_send)
-    all_out(ca_ref.at[1:DP], t3_send)
+    all_out(ca_ref.at[1:DP, :, 0:256], t3_send)
     all_out(q0_ref, rs_send.at[0])
     all_out(q1_ref, rs_send.at[1])
     all_out(q2_ref, rs_send.at[2])

time: 72.6 us -> 72.2 us (level)
  no operation moved by 1% of the time
where the time goes in v4:
time: 72.2 us; the launch traced here: 72.1 us
  Pallas kernels  71.4 us (99%)
    pallas_call x1, Pallas kernels, shards(): pl.pallas_call(kernel, out_shape=(pltpu.VMEM((ROWS, D), F32), pltpu.VMEM(...  68.2 us
    pallas_call x1, Pallas kernels, shards(): pl.pallas_call(ship, out_shape=(jax.ShapeDtypeStruct((ROWS, D), F32), jax...  3.23 us

profile of v4, /device:TPU:0, one launch (start us, length us, event | category | flops | bytes accessed | tf_op | source)
XLA Modules:
  0.0 72.1 jit_solution(15783693764801415728)
XLA Ops:
  0.6 68.2 %head.1 = (f32[2048,768]{1,0:T(8,128)S(1)}, f32[16,768]{1,0:T(8,128)S(1)}, f32[1,128]{1,0:T(1,128)S(1)}) custom-call(bf16[128,768]{1,0:T(8,128)(2,1)} %docs_hbm.1, bf16[2048,768]{1,0:T(8,128)(2,1)} %labels_hbm.1, s32[16,1,17]{2,1,0:T(1,128)} %bitcast.1, s32[16,17]{1,0:T(8,128)} %row_hbm.1), custom_call_target="tpu_custom_call" | custom-call | flops 25769803776 | bytes 15728640 | tf_op jit(solution)/shard_map/head/pallas_call | solution.py:713
  68.8 3.2 %ship.1 = (f32[2048,768]{1,0:T(8,128)}, f32[16,768]{1,0:T(8,128)}, f32[16]{0:T(128)}) custom-call(f32[2048,768]{1,0:T(8,128)S(1)} %get-tuple-element.9.lg_in, f32[16,768]{1,0:T(8,128)S(1)} %get-tuple-element.10.dg_in, f32[1,128]{1,0:T(1,128)S(1)} %get-tuple-element.11.loss_in), custom_call_target="tpu_custom_call" | custom-call | tf_op jit(solution)/shard_map/ship/pallas_call | solution.py:774

commit v5 on v4

--- a/solution.py
+++ b/solution.py
@@ -658,9 +658,6 @@
         @pl.when(r == 1)
         def _():
             ring_relay(0)
-
-        @pl.when(r == 2)
-        def _():
             ring_relay(1)
 
         @pl.when(r == 4)

time: 72.2 us -> 72.2 us (level)
  no operation moved by 1% of the time
where the time goes in v5:
time: 72.2 us; the launch traced here: 72.1 us
  Pallas kernels  71.4 us (99%)
    pallas_call x1, Pallas kernels, shards(): pl.pallas_call(kernel, out_shape=(pltpu.VMEM((ROWS, D), F32), pltpu.VMEM(...  68.2 us
    pallas_call x1, Pallas kernels, shards(): pl.pallas_call(ship, out_shape=(jax.ShapeDtypeStruct((ROWS, D), F32), jax...  3.23 us

profile of v5, /device:TPU:0, one launch (start us, length us, event | category | flops | bytes accessed | tf_op | source)
XLA Modules:
  0.0 72.1 jit_solution(7313173638923896221)
XLA Ops:
  0.6 68.2 %head.1 = (f32[2048,768]{1,0:T(8,128)S(1)}, f32[16,768]{1,0:T(8,128)S(1)}, f32[1,128]{1,0:T(1,128)S(1)}) custom-call(bf16[128,768]{1,0:T(8,128)(2,1)} %docs_hbm.1, bf16[2048,768]{1,0:T(8,128)(2,1)} %labels_hbm.1, s32[16,1,17]{2,1,0:T(1,128)} %bitcast.1, s32[16,17]{1,0:T(8,128)} %row_hbm.1), custom_call_target="tpu_custom_call" | custom-call | flops 25769803776 | bytes 15728640 | tf_op jit(solution)/shard_map/head/pallas_call | solution.py:710
  68.8 3.2 %ship.1 = (f32[2048,768]{1,0:T(8,128)}, f32[16,768]{1,0:T(8,128)}, f32[16]{0:T(128)}) custom-call(f32[2048,768]{1,0:T(8,128)S(1)} %get-tuple-element.9.lg_in, f32[16,768]{1,0:T(8,128)S(1)} %get-tuple-element.10.dg_in, f32[1,128]{1,0:T(1,128)S(1)} %get-tuple-element.11.loss_in), custom_call_target="tpu_custom_call" | custom-call | tf_op jit(solution)/shard_map/ship/pallas_call | solution.py:771

commit v6 on v4

--- a/solution.py
+++ b/solution.py
@@ -397,6 +397,10 @@
             for k in (1, 2, 3):
                 take(k)
 
+        @pl.when(i == 1)
+        def _():
+            take(4)
+
         @pl.when(i == 2)
         def _():
             find()
@@ -420,10 +424,6 @@
             each(0, 8, flip)
 
         top = score_step(i * 2 + 1, 1, top)
-
-        @pl.when(i == 1)
-        def _():
-            take(4)
 
         return top
 

time: 72.2 us -> 71.1 us (0.985)
  Pallas kernels: 71.4 us -> 70.1 us
    pallas_call x1, Pallas kernels: 68.2 us -> 66.9 us  [shards(): pl.pallas_call(kernel, out_shape=(pltpu.VMEM((ROWS, D), F32), pltpu.VMEM(...]
where the time goes in v6:
time: 71.1 us; the launch traced here: 70.8 us
  Pallas kernels  70.1 us (99%)
    pallas_call x1, Pallas kernels, shards(): pl.pallas_call(kernel, out_shape=(pltpu.VMEM((ROWS, D), F32), pltpu.VMEM(...  66.9 us
    pallas_call x1, Pallas kernels, shards(): pl.pallas_call(ship, out_shape=(jax.ShapeDtypeStruct((ROWS, D), F32), jax...  3.23 us

profile of v6, /device:TPU:0, one launch (start us, length us, event | category | flops | bytes accessed | tf_op | source)
XLA Modules:
  0.0 70.8 jit_solution(2281481585313255821)
XLA Ops:
  0.6 66.9 %head.1 = (f32[2048,768]{1,0:T(8,128)S(1)}, f32[16,768]{1,0:T(8,128)S(1)}, f32[1,128]{1,0:T(1,128)S(1)}) custom-call(bf16[128,768]{1,0:T(8,128)(2,1)} %docs_hbm.1, bf16[2048,768]{1,0:T(8,128)(2,1)} %labels_hbm.1, s32[16,1,17]{2,1,0:T(1,128)} %bitcast.1, s32[16,17]{1,0:T(8,128)} %row_hbm.1), custom_call_target="tpu_custom_call" | custom-call | flops 25769803776 | bytes 15728640 | tf_op jit(solution)/shard_map/head/pallas_call | solution.py:713
  67.5 3.2 %ship.1 = (f32[2048,768]{1,0:T(8,128)}, f32[16,768]{1,0:T(8,128)}, f32[16]{0:T(128)}) custom-call(f32[2048,768]{1,0:T(8,128)S(1)} %get-tuple-element.9.lg_in, f32[16,768]{1,0:T(8,128)S(1)} %get-tuple-element.10.dg_in, f32[1,128]{1,0:T(1,128)S(1)} %get-tuple-element.11.loss_in), custom_call_target="tpu_custom_call" | custom-call | tf_op jit(solution)/shard_map/ship/pallas_call | solution.py:774
